TPU v7x, 256 devices: a whole 4x4x8 slice. The times are simulated.
256 devices in a mesh: wide: 64 (over y, z, core), rep: 4 (over x).
Axes of the slice: x: 4, y: 4, z: 8, core: 2. Of those that a mesh axis runs over, the one named last changes fastest.
Arguments:
- pooled_emb: bfloat16 [2048, 39, 64], P(('wide', 'rep')), may hold values from -6 to 6
- conv_weight: float32 [14, 7], replicated, may hold values from -2 to 2
- conv_bias: float32 [14], replicated, may hold values from -3 to 3
- rec_weight: float32 [14, 19, 57], replicated, may hold values from -0.375 to 0.375
- rec_bias: float32 [57], replicated, may hold values from -3 to 3
- feat_cot: bfloat16 [2048, 96, 64], P(('wide', 'rep')), may hold values from -6 to 6
- gram_cot: bfloat16 [2048, 96, 96], P(('wide', 'rep')), may hold values from -0.59765625 to 0.59765625
- bag_ids: int32 [2048, 39, 4], P(('wide', 'rep')), may hold values from 0 to 32767, as said below
- bag_lengths: int32 [2048, 39], P(('wide', 'rep')), may hold values from 1 to 4
- field_table: int32 [39], replicated, may hold values from 0 to 25
Outputs:
- table_grad: float32 [26, 64, 32768], P(None, None, ('wide', 'rep'))
- conv_weight_grad: float32 [14, 7], replicated
- conv_bias_grad: float32 [14], replicated
- rec_weight_grad: float32 [14, 19, 57], replicated
- rec_bias_grad: float32 [57], replicated
Inputs may be any that keep to these rules, and one draw needn't show every extreme that they name: `bag_ids`: each table's rows fall into 64 equal owner ranges of 512 rows. Counting live slots only, one device's samples name at most 39 rows of one owner range; one owner range receives exactly 39 from every device, and each device's other live lookups spread over the remaining owner ranges with counts that differ by at most one. Ids in slots past a bag's length are arbitrary rows.
All inputs are finite; a program needn't handle non-finite values.
Results may differ from a plain program's by a relative error of at most 0.0029.
Values may be sent and summed in bfloat16 or wider, within the bound.
A program may use at most 64 MiB of HBM per device.

v0:
```python
import math

import jax
import jax.numpy as jnp
from jax import lax
from jax.sharding import PartitionSpec as P

K = 64
F = 39
NT = 26
C = 14
KH = 7
BAG = 4
T_SHARE = 128
P_SIZE = 19


def dense_backward(emb_block, cot_block, gram_block, conv_weight, conv_bias, rec_weight, rec_bias):
    highest = lax.Precision.HIGHEST
    fields = emb_block.astype(jnp.float32)
    margin = (KH - 1) // 2
    padded = jnp.pad(fields, ((0, 0), (margin, margin), (0, 0)))
    shifted = jnp.stack([padded[:, shift : shift + F, :] for shift in range(KH)], axis=1)
    conv_out = (
        jnp.einsum("cd,bdik->bcik", conv_weight, shifted, precision=highest)
        + conv_bias[None, :, None, None]
    )
    activated = jnp.tanh(conv_out)
    pair_maps = activated[:, :, : 2 * P_SIZE, :].reshape(activated.shape[0], C, P_SIZE, 2, K)
    pooled = 0.5 * (pair_maps[:, :, :, 0, :] + pair_maps[:, :, :, 1, :])
    recombined = (
        jnp.einsum("bcpk,cpn->bnk", pooled, rec_weight, precision=highest) + rec_bias[None, :, None]
    )
    new_maps = jnp.tanh(recombined)
    features = jnp.concatenate([fields, new_maps], axis=1)
    gram_grad = gram_block.astype(jnp.float32)
    symmetric = gram_grad + jnp.swapaxes(gram_grad, 1, 2)
    feat_grad = cot_block.astype(jnp.float32) + jnp.einsum(
        "bij,bjk->bik", symmetric, features, precision=highest
    )
    recomb_grad = feat_grad[:, F:, :] * (1.0 - new_maps * new_maps)
    rec_weight_term = jnp.einsum("bcpk,bnk->cpn", pooled, recomb_grad, precision=highest)
    rec_bias_term = jnp.sum(recomb_grad, axis=(0, 2))
    pooled_grad = jnp.einsum("cpn,bnk->bcpk", rec_weight, recomb_grad, precision=highest)
    tanh_grad = jnp.repeat(0.5 * pooled_grad, 2, axis=2)
    tanh_grad = jnp.pad(tanh_grad, ((0, 0), (0, 0), (0, F - 2 * P_SIZE), (0, 0)))
    conv_grad = tanh_grad * (1.0 - activated * activated)
    conv_weight_term = jnp.einsum("bcik,bdik->cd", conv_grad, shifted, precision=highest)
    conv_bias_term = jnp.sum(conv_grad, axis=(0, 2, 3))
    grad_padded = jnp.pad(conv_grad, ((0, 0), (0, 0), (margin, margin), (0, 0)))
    field_grad = feat_grad[:, :F, :]
    for shift in range(KH):
        window = grad_padded[:, :, KH - 1 - shift : KH - 1 - shift + F, :]
        field_grad = field_grad + jnp.einsum(
            "c,bcik->bik", conv_weight[:, shift], window, precision=highest
        )
    return (
        field_grad.astype(jnp.bfloat16),
        (conv_weight_term, conv_bias_term, rec_weight_term, rec_bias_term),
    )


def dense_in_blocks(pooled_emb, feat_cot, gram_cot, conv_weight, conv_bias, rec_weight, rec_bias):
    local_samples = pooled_emb.shape[0]
    block_rows = math.gcd(local_samples, 32)
    block_count = local_samples // block_rows

    def one_block(packed):
        return dense_backward(
            packed[0], packed[1], packed[2], conv_weight, conv_bias, rec_weight, rec_bias
        )

    stacked = (
        pooled_emb.reshape((block_count, block_rows) + pooled_emb.shape[1:]),
        feat_cot.reshape((block_count, block_rows) + feat_cot.shape[1:]),
        gram_cot.reshape((block_count, block_rows) + gram_cot.shape[1:]),
    )
    emb_grad, terms = lax.map(one_block, stacked)
    emb_grad = emb_grad.reshape(pooled_emb.shape)
    terms = tuple((jnp.sum(term, axis=0) for term in terms))
    return (emb_grad, terms)


def slot_rows(row_ids, lengths, field_table, own_rows):
    live_slot = jnp.arange(row_ids.shape[-1], dtype=jnp.int32)[None, None, :] < lengths[:, :, None]
    row_index = field_table[None, :, None] * own_rows + row_ids % own_rows
    return (live_slot, row_ids // own_rows, row_index)


def spread_slots(emb_grad, slot_width):
    rows_here, fields_here, columns = emb_grad.shape
    return jnp.broadcast_to(
        emb_grad[:, :, None, :], (rows_here, fields_here, slot_width, columns)
    ).reshape(-1, columns)


def local(
    pooled_emb,
    conv_weight,
    conv_bias,
    rec_weight,
    rec_bias,
    feat_cot,
    gram_cot,
    bag_ids,
    bag_lengths,
    field_table,
):
    wide_size = lax.axis_size("wide")
    rep_size = lax.axis_size("rep")
    own_rows = rep_size * T_SHARE
    stripe = NT * own_rows
    local_samples = pooled_emb.shape[0]
    emb_grad, dense_terms = dense_in_blocks(
        pooled_emb, feat_cot, gram_cot, conv_weight, conv_bias, rec_weight, rec_bias
    )
    dense_sums = lax.psum(dense_terms, ("wide", "rep"))
    grad_scale = 1.0 / math.sqrt(local_samples * wide_size * rep_size)
    owner_index = lax.axis_index("wide")
    empty_slab = jnp.zeros((stripe + 1, K), jnp.float32)
    group_ids, group_lengths = (
        lax.all_gather(bag_ids, "wide", axis=0, tiled=True),
        lax.all_gather(bag_lengths, "wide", axis=0, tiled=True),
    )
    shard_grad = lax.all_gather(emb_grad, "wide", axis=0, tiled=True)
    piece_rows = shard_grad.shape[0]
    block_rows = math.gcd(piece_rows, local_samples)

    def add_block(block_num, partial_value):
        offset = block_num * block_rows
        ids_here = lax.dynamic_slice_in_dim(group_ids, offset, block_rows, 0)
        lengths_here = lax.dynamic_slice_in_dim(group_lengths, offset, block_rows, 0)
        grad_here = lax.dynamic_slice_in_dim(shard_grad, offset, block_rows, 0)
        live_slot, owner_of, row_index = slot_rows(ids_here, lengths_here, field_table, own_rows)
        target = jnp.where(live_slot & (owner_of == owner_index), row_index, stripe)
        return partial_value.at[target.reshape(-1)].add(
            spread_slots(grad_here, BAG).astype(jnp.float32)
        )

    row_slab = lax.fori_loop(0, piece_rows // block_rows, add_block, empty_slab)
    owned_rows = row_slab[:stripe].reshape(NT, own_rows, K).transpose(0, 2, 1)
    table_grad = lax.psum_scatter(owned_rows, "rep", scatter_dimension=2, tiled=True)
    conv_weight_sum, conv_bias_sum, rec_weight_sum, rec_bias_sum = dense_sums
    return (
        table_grad,
        conv_weight_sum * grad_scale,
        conv_bias_sum * grad_scale,
        rec_weight_sum * grad_scale,
        rec_bias_sum * grad_scale,
    )


def solution(mesh):
    in_specs = (
        P(("wide", "rep"), None, None),
        P(),
        P(),
        P(),
        P(),
        P(("wide", "rep"), None, None),
        P(("wide", "rep"), None, None),
        P(("wide", "rep"), None, None),
        P(("wide", "rep"), None),
        P(),
    )
    out_specs = (P(None, None, ("wide", "rep")), P(), P(), P(), P())
    return jax.shard_map(local, mesh=mesh, in_specs=in_specs, out_specs=out_specs, check_vma=False)
```

profile of v0, /device:TPU:1, one launch (start us, length us, event | category | flops | bytes accessed | tf_op | source)
XLA Modules:
  0.0 1502.6 jit_solution(18098622875494623771)
XLA Ops:
  51.6 52.0 %all_gather.9 = s32[512,39]{1,0:T(8,128)} all-gather(s32[8,39]{1,0:T(8,128)S(1)} %copy-done.13), channel_id=1, replica_groups=mesh['wide'=64,'rep'=4] {'wide'}, dimensions={0}, use_global_device_ids=true | all-gather | bytes 81120 | tf_op jit(solution)/shard_map/all_gather | solution.py:123
  103.7 54.2 %all_gather.10 = s32[512,39,4]{1,2,0:T(4,128)} all-gather(s32[8,39,4]{1,2,0:T(4,128)S(1)} %copy-done.12), channel_id=1, replica_groups=mesh['wide'=64,'rep'=4] {'wide'}, dimensions={0}, use_global_device_ids=true | all-gather | bytes 324480 | tf_op jit(solution)/shard_map/all_gather | solution.py:122
  160.9 1231.3 %while.10 = (s32[]{:T(128)}, f32[13313,64]{1,0:T(8,128)}, s32[512,39]{1,0:T(8,128)}, s32[512,39,4]{1,2,0:T(4,128)}, s32[]{:T(128)}, /*index=5*/s32[39]{0:T(128)S...) while((s32[]{:T(128)}, f32[13313,64]{1,0:T(8,128)}, ...), condition=%wide.region_2.3_spmd, body=%wide.region_0.2_spmd.sunk | while | flops 133581 | bytes 1616799 | solution.py:140
  163.9 16.3 %scatter_fusion = f32[13313,64]{1,0:T(8,128)} fusion(f32[13313,64]{1,0:T(8,128)} %get-tuple-element.429, s32[1248]{0:T(1024)S(1)} %fusion.78, f32[1248,64]{1,0:T(8,128)S(1)} %bitcast.139), kind=kCustom, calls=%fused_computation.clone.1 | custom fusion | flops 79872 | bytes 963456 | tf_op jit(solution)/shard_map/while/body/eval_jaxpr/scatter-add | solution.py:136
  221.6 16.3 %scatter_fusion = f32[13313,64]{1,0:T(8,128)} fusion(f32[13313,64]{1,0:T(8,128)} %get-tuple-element.429, s32[1248]{0:T(1024)S(1)} %fusion.78, f32[1248,64]{1,0:T(8,128)S(1)} %bitcast.139), kind=kCustom, calls=%fused_computation.clone.1 | custom fusion | flops 79872 | bytes 963456 | tf_op jit(solution)/shard_map/while/body/eval_jaxpr/scatter-add | solution.py:136
  240.8 16.3 %scatter_fusion = f32[13313,64]{1,0:T(8,128)} fusion(f32[13313,64]{1,0:T(8,128)} %get-tuple-element.429, s32[1248]{0:T(1024)S(1)} %fusion.78, f32[1248,64]{1,0:T(8,128)S(1)} %bitcast.139), kind=kCustom, calls=%fused_computation.clone.1 | custom fusion | flops 79872 | bytes 963456 | tf_op jit(solution)/shard_map/while/body/eval_jaxpr/scatter-add | solution.py:136
  260.1 16.3 %scatter_fusion = f32[13313,64]{1,0:T(8,128)} fusion(f32[13313,64]{1,0:T(8,128)} %get-tuple-element.429, s32[1248]{0:T(1024)S(1)} %fusion.78, f32[1248,64]{1,0:T(8,128)S(1)} %bitcast.139), kind=kCustom, calls=%fused_computation.clone.1 | custom fusion | flops 79872 | bytes 963456 | tf_op jit(solution)/shard_map/while/body/eval_jaxpr/scatter-add | solution.py:136
  279.3 16.3 %scatter_fusion = f32[13313,64]{1,0:T(8,128)} fusion(f32[13313,64]{1,0:T(8,128)} %get-tuple-element.429, s32[1248]{0:T(1024)S(1)} %fusion.78, f32[1248,64]{1,0:T(8,128)S(1)} %bitcast.139), kind=kCustom, calls=%fused_computation.clone.1 | custom fusion | flops 79872 | bytes 963456 | tf_op jit(solution)/shard_map/while/body/eval_jaxpr/scatter-add | solution.py:136
  298.5 16.3 %scatter_fusion = f32[13313,64]{1,0:T(8,128)} fusion(f32[13313,64]{1,0:T(8,128)} %get-tuple-element.429, s32[1248]{0:T(1024)S(1)} %fusion.78, f32[1248,64]{1,0:T(8,128)S(1)} %bitcast.139), kind=kCustom, calls=%fused_computation.clone.1 | custom fusion | flops 79872 | bytes 963456 | tf_op jit(solution)/shard_map/while/body/eval_jaxpr/scatter-add | solution.py:136
  317.8 16.3 %scatter_fusion = f32[13313,64]{1,0:T(8,128)} fusion(f32[13313,64]{1,0:T(8,128)} %get-tuple-element.429, s32[1248]{0:T(1024)S(1)} %fusion.78, f32[1248,64]{1,0:T(8,128)S(1)} %bitcast.139), kind=kCustom, calls=%fused_computation.clone.1 | custom fusion | flops 79872 | bytes 963456 | tf_op jit(solution)/shard_map/while/body/eval_jaxpr/scatter-add | solution.py:136
  337.0 16.3 %scatter_fusion = f32[13313,64]{1,0:T(8,128)} fusion(f32[13313,64]{1,0:T(8,128)} %get-tuple-element.429, s32[1248]{0:T(1024)S(1)} %fusion.78, f32[1248,64]{1,0:T(8,128)S(1)} %bitcast.139), kind=kCustom, calls=%fused_computation.clone.1 | custom fusion | flops 79872 | bytes 963456 | tf_op jit(solution)/shard_map/while/body/eval_jaxpr/scatter-add | solution.py:136
  356.3 16.3 %scatter_fusion = f32[13313,64]{1,0:T(8,128)} fusion(f32[13313,64]{1,0:T(8,128)} %get-tuple-element.429, s32[1248]{0:T(1024)S(1)} %fusion.78, f32[1248,64]{1,0:T(8,128)S(1)} %bitcast.139), kind=kCustom, calls=%fused_computation.clone.1 | custom fusion | flops 79872 | bytes 963456 | tf_op jit(solution)/shard_map/while/body/eval_jaxpr/scatter-add | solution.py:136
  394.7 16.3 %scatter_fusion = f32[13313,64]{1,0:T(8,128)} fusion(f32[13313,64]{1,0:T(8,128)} %get-tuple-element.429, s32[1248]{0:T(1024)S(1)} %fusion.78, f32[1248,64]{1,0:T(8,128)S(1)} %bitcast.139), kind=kCustom, calls=%fused_computation.clone.1 | custom fusion | flops 79872 | bytes 963456 | tf_op jit(solution)/shard_map/while/body/eval_jaxpr/scatter-add | solution.py:136
  414.0 16.3 %scatter_fusion = f32[13313,64]{1,0:T(8,128)} fusion(f32[13313,64]{1,0:T(8,128)} %get-tuple-element.429, s32[1248]{0:T(1024)S(1)} %fusion.78, f32[1248,64]{1,0:T(8,128)S(1)} %bitcast.139), kind=kCustom, calls=%fused_computation.clone.1 | custom fusion | flops 79872 | bytes 963456 | tf_op jit(solution)/shard_map/while/body/eval_jaxpr/scatter-add | solution.py:136
  433.2 16.3 %scatter_fusion = f32[13313,64]{1,0:T(8,128)} fusion(f32[13313,64]{1,0:T(8,128)} %get-tuple-element.429, s32[1248]{0:T(1024)S(1)} %fusion.78, f32[1248,64]{1,0:T(8,128)S(1)} %bitcast.139), kind=kCustom, calls=%fused_computation.clone.1 | custom fusion | flops 79872 | bytes 963456 | tf_op jit(solution)/shard_map/while/body/eval_jaxpr/scatter-add | solution.py:136
  452.5 16.3 %scatter_fusion = f32[13313,64]{1,0:T(8,128)} fusion(f32[13313,64]{1,0:T(8,128)} %get-tuple-element.429, s32[1248]{0:T(1024)S(1)} %fusion.78, f32[1248,64]{1,0:T(8,128)S(1)} %bitcast.139), kind=kCustom, calls=%fused_computation.clone.1 | custom fusion | flops 79872 | bytes 963456 | tf_op jit(solution)/shard_map/while/body/eval_jaxpr/scatter-add | solution.py:136
  471.7 16.3 %scatter_fusion = f32[13313,64]{1,0:T(8,128)} fusion(f32[13313,64]{1,0:T(8,128)} %get-tuple-element.429, s32[1248]{0:T(1024)S(1)} %fusion.78, f32[1248,64]{1,0:T(8,128)S(1)} %bitcast.139), kind=kCustom, calls=%fused_computation.clone.1 | custom fusion | flops 79872 | bytes 963456 | tf_op jit(solution)/shard_map/while/body/eval_jaxpr/scatter-add | solution.py:136
  490.9 16.3 %scatter_fusion = f32[13313,64]{1,0:T(8,128)} fusion(f32[13313,64]{1,0:T(8,128)} %get-tuple-element.429, s32[1248]{0:T(1024)S(1)} %fusion.78, f32[1248,64]{1,0:T(8,128)S(1)} %bitcast.139), kind=kCustom, calls=%fused_computation.clone.1 | custom fusion | flops 79872 | bytes 963456 | tf_op jit(solution)/shard_map/while/body/eval_jaxpr/scatter-add | solution.py:136
  548.7 16.3 %scatter_fusion = f32[13313,64]{1,0:T(8,128)} fusion(f32[13313,64]{1,0:T(8,128)} %get-tuple-element.429, s32[1248]{0:T(1024)S(1)} %fusion.78, f32[1248,64]{1,0:T(8,128)S(1)} %bitcast.139), kind=kCustom, calls=%fused_computation.clone.1 | custom fusion | flops 79872 | bytes 963456 | tf_op jit(solution)/shard_map/while/body/eval_jaxpr/scatter-add | solution.py:136
  587.1 16.3 %scatter_fusion = f32[13313,64]{1,0:T(8,128)} fusion(f32[13313,64]{1,0:T(8,128)} %get-tuple-element.429, s32[1248]{0:T(1024)S(1)} %fusion.78, f32[1248,64]{1,0:T(8,128)S(1)} %bitcast.139), kind=kCustom, calls=%fused_computation.clone.1 | custom fusion | flops 79872 | bytes 963456 | tf_op jit(solution)/shard_map/while/body/eval_jaxpr/scatter-add | solution.py:136
  606.4 16.3 %scatter_fusion = f32[13313,64]{1,0:T(8,128)} fusion(f32[13313,64]{1,0:T(8,128)} %get-tuple-element.429, s32[1248]{0:T(1024)S(1)} %fusion.78, f32[1248,64]{1,0:T(8,128)S(1)} %bitcast.139), kind=kCustom, calls=%fused_computation.clone.1 | custom fusion | flops 79872 | bytes 963456 | tf_op jit(solution)/shard_map/while/body/eval_jaxpr/scatter-add | solution.py:136
  625.6 16.3 %scatter_fusion = f32[13313,64]{1,0:T(8,128)} fusion(f32[13313,64]{1,0:T(8,128)} %get-tuple-element.429, s32[1248]{0:T(1024)S(1)} %fusion.78, f32[1248,64]{1,0:T(8,128)S(1)} %bitcast.139), kind=kCustom, calls=%fused_computation.clone.1 | custom fusion | flops 79872 | bytes 963456 | tf_op jit(solution)/shard_map/while/body/eval_jaxpr/scatter-add | solution.py:136
  644.9 16.3 %scatter_fusion = f32[13313,64]{1,0:T(8,128)} fusion(f32[13313,64]{1,0:T(8,128)} %get-tuple-element.429, s32[1248]{0:T(1024)S(1)} %fusion.78, f32[1248,64]{1,0:T(8,128)S(1)} %bitcast.139), kind=kCustom, calls=%fused_computation.clone.1 | custom fusion | flops 79872 | bytes 963456 | tf_op jit(solution)/shard_map/while/body/eval_jaxpr/scatter-add | solution.py:136
  664.1 16.3 %scatter_fusion = f32[13313,64]{1,0:T(8,128)} fusion(f32[13313,64]{1,0:T(8,128)} %get-tuple-element.429, s32[1248]{0:T(1024)S(1)} %fusion.78, f32[1248,64]{1,0:T(8,128)S(1)} %bitcast.139), kind=kCustom, calls=%fused_computation.clone.1 | custom fusion | flops 79872 | bytes 963456 | tf_op jit(solution)/shard_map/while/body/eval_jaxpr/scatter-add | solution.py:136
  683.3 16.3 %scatter_fusion = f32[13313,64]{1,0:T(8,128)} fusion(f32[13313,64]{1,0:T(8,128)} %get-tuple-element.429, s32[1248]{0:T(1024)S(1)} %fusion.78, f32[1248,64]{1,0:T(8,128)S(1)} %bitcast.139), kind=kCustom, calls=%fused_computation.clone.1 | custom fusion | flops 79872 | bytes 963456 | tf_op jit(solution)/shard_map/while/body/eval_jaxpr/scatter-add | solution.py:136
  702.6 16.3 %scatter_fusion = f32[13313,64]{1,0:T(8,128)} fusion(f32[13313,64]{1,0:T(8,128)} %get-tuple-element.429, s32[1248]{0:T(1024)S(1)} %fusion.78, f32[1248,64]{1,0:T(8,128)S(1)} %bitcast.139), kind=kCustom, calls=%fused_computation.clone.1 | custom fusion | flops 79872 | bytes 963456 | tf_op jit(solution)/shard_map/while/body/eval_jaxpr/scatter-add | solution.py:136
  760.3 16.3 %scatter_fusion = f32[13313,64]{1,0:T(8,128)} fusion(f32[13313,64]{1,0:T(8,128)} %get-tuple-element.429, s32[1248]{0:T(1024)S(1)} %fusion.78, f32[1248,64]{1,0:T(8,128)S(1)} %bitcast.139), kind=kCustom, calls=%fused_computation.clone.1 | custom fusion | flops 79872 | bytes 963456 | tf_op jit(solution)/shard_map/while/body/eval_jaxpr/scatter-add | solution.py:136
  779.5 16.3 %scatter_fusion = f32[13313,64]{1,0:T(8,128)} fusion(f32[13313,64]{1,0:T(8,128)} %get-tuple-element.429, s32[1248]{0:T(1024)S(1)} %fusion.78, f32[1248,64]{1,0:T(8,128)S(1)} %bitcast.139), kind=kCustom, calls=%fused_computation.clone.1 | custom fusion | flops 79872 | bytes 963456 | tf_op jit(solution)/shard_map/while/body/eval_jaxpr/scatter-add | solution.py:136
  818.0 16.3 %scatter_fusion = f32[13313,64]{1,0:T(8,128)} fusion(f32[13313,64]{1,0:T(8,128)} %get-tuple-element.429, s32[1248]{0:T(1024)S(1)} %fusion.78, f32[1248,64]{1,0:T(8,128)S(1)} %bitcast.139), kind=kCustom, calls=%fused_computation.clone.1 | custom fusion | flops 79872 | bytes 963456 | tf_op jit(solution)/shard_map/while/body/eval_jaxpr/scatter-add | solution.py:136
  837.2 16.3 %scatter_fusion = f32[13313,64]{1,0:T(8,128)} fusion(f32[13313,64]{1,0:T(8,128)} %get-tuple-element.429, s32[1248]{0:T(1024)S(1)} %fusion.78, f32[1248,64]{1,0:T(8,128)S(1)} %bitcast.139), kind=kCustom, calls=%fused_computation.clone.1 | custom fusion | flops 79872 | bytes 963456 | tf_op jit(solution)/shard_map/while/body/eval_jaxpr/scatter-add | solution.py:136
  856.5 16.3 %scatter_fusion = f32[13313,64]{1,0:T(8,128)} fusion(f32[13313,64]{1,0:T(8,128)} %get-tuple-element.429, s32[1248]{0:T(1024)S(1)} %fusion.78, f32[1248,64]{1,0:T(8,128)S(1)} %bitcast.139), kind=kCustom, calls=%fused_computation.clone.1 | custom fusion | flops 79872 | bytes 963456 | tf_op jit(solution)/shard_map/while/body/eval_jaxpr/scatter-add | solution.py:136
  875.7 16.3 %scatter_fusion = f32[13313,64]{1,0:T(8,128)} fusion(f32[13313,64]{1,0:T(8,128)} %get-tuple-element.429, s32[1248]{0:T(1024)S(1)} %fusion.78, f32[1248,64]{1,0:T(8,128)S(1)} %bitcast.139), kind=kCustom, calls=%fused_computation.clone.1 | custom fusion | flops 79872 | bytes 963456 | tf_op jit(solution)/shard_map/while/body/eval_jaxpr/scatter-add | solution.py:136
  894.9 16.3 %scatter_fusion = f32[13313,64]{1,0:T(8,128)} fusion(f32[13313,64]{1,0:T(8,128)} %get-tuple-element.429, s32[1248]{0:T(1024)S(1)} %fusion.78, f32[1248,64]{1,0:T(8,128)S(1)} %bitcast.139), kind=kCustom, calls=%fused_computation.clone.1 | custom fusion | flops 79872 | bytes 963456 | tf_op jit(solution)/shard_map/while/body/eval_jaxpr/scatter-add | solution.py:136
  914.2 16.3 %scatter_fusion = f32[13313,64]{1,0:T(8,128)} fusion(f32[13313,64]{1,0:T(8,128)} %get-tuple-element.429, s32[1248]{0:T(1024)S(1)} %fusion.78, f32[1248,64]{1,0:T(8,128)S(1)} %bitcast.139), kind=kCustom, calls=%fused_computation.clone.1 | custom fusion | flops 79872 | bytes 963456 | tf_op jit(solution)/shard_map/while/body/eval_jaxpr/scatter-add | solution.py:136
  933.4 16.3 %scatter_fusion = f32[13313,64]{1,0:T(8,128)} fusion(f32[13313,64]{1,0:T(8,128)} %get-tuple-element.429, s32[1248]{0:T(1024)S(1)} %fusion.78, f32[1248,64]{1,0:T(8,128)S(1)} %bitcast.139), kind=kCustom, calls=%fused_computation.clone.1 | custom fusion | flops 79872 | bytes 963456 | tf_op jit(solution)/shard_map/while/body/eval_jaxpr/scatter-add | solution.py:136
  971.9 16.3 %scatter_fusion = f32[13313,64]{1,0:T(8,128)} fusion(f32[13313,64]{1,0:T(8,128)} %get-tuple-element.429, s32[1248]{0:T(1024)S(1)} %fusion.78, f32[1248,64]{1,0:T(8,128)S(1)} %bitcast.139), kind=kCustom, calls=%fused_computation.clone.1 | custom fusion | flops 79872 | bytes 963456 | tf_op jit(solution)/shard_map/while/body/eval_jaxpr/scatter-add | solution.py:136
  991.2 16.3 %scatter_fusion = f32[13313,64]{1,0:T(8,128)} fusion(f32[13313,64]{1,0:T(8,128)} %get-tuple-element.429, s32[1248]{0:T(1024)S(1)} %fusion.78, f32[1248,64]{1,0:T(8,128)S(1)} %bitcast.139), kind=kCustom, calls=%fused_computation.clone.1 | custom fusion | flops 79872 | bytes 963456 | tf_op jit(solution)/shard_map/while/body/eval_jaxpr/scatter-add | solution.py:136
  1010.4 16.3 %scatter_fusion = f32[13313,64]{1,0:T(8,128)} fusion(f32[13313,64]{1,0:T(8,128)} %get-tuple-element.429, s32[1248]{0:T(1024)S(1)} %fusion.78, f32[1248,64]{1,0:T(8,128)S(1)} %bitcast.139), kind=kCustom, calls=%fused_computation.clone.1 | custom fusion | flops 79872 | bytes 963456 | tf_op jit(solution)/shard_map/while/body/eval_jaxpr/scatter-add | solution.py:136
  1029.7 16.3 %scatter_fusion = f32[13313,64]{1,0:T(8,128)} fusion(f32[13313,64]{1,0:T(8,128)} %get-tuple-element.429, s32[1248]{0:T(1024)S(1)} %fusion.78, f32[1248,64]{1,0:T(8,128)S(1)} %bitcast.139), kind=kCustom, calls=%fused_computation.clone.1 | custom fusion | flops 79872 | bytes 963456 | tf_op jit(solution)/shard_map/while/body/eval_jaxpr/scatter-add | solution.py:136
  1068.1 16.3 %scatter_fusion = f32[13313,64]{1,0:T(8,128)} fusion(f32[13313,64]{1,0:T(8,128)} %get-tuple-element.429, s32[1248]{0:T(1024)S(1)} %fusion.78, f32[1248,64]{1,0:T(8,128)S(1)} %bitcast.139), kind=kCustom, calls=%fused_computation.clone.1 | custom fusion | flops 79872 | bytes 963456 | tf_op jit(solution)/shard_map/while/body/eval_jaxpr/scatter-add | solution.py:136
  1087.4 16.3 %scatter_fusion = f32[13313,64]{1,0:T(8,128)} fusion(f32[13313,64]{1,0:T(8,128)} %get-tuple-element.429, s32[1248]{0:T(1024)S(1)} %fusion.78, f32[1248,64]{1,0:T(8,128)S(1)} %bitcast.139), kind=kCustom, calls=%fused_computation.clone.1 | custom fusion | flops 79872 | bytes 963456 | tf_op jit(solution)/shard_map/while/body/eval_jaxpr/scatter-add | solution.py:136
  1125.9 16.3 %scatter_fusion = f32[13313,64]{1,0:T(8,128)} fusion(f32[13313,64]{1,0:T(8,128)} %get-tuple-element.429, s32[1248]{0:T(1024)S(1)} %fusion.78, f32[1248,64]{1,0:T(8,128)S(1)} %bitcast.139), kind=kCustom, calls=%fused_computation.clone.1 | custom fusion | flops 79872 | bytes 963456 | tf_op jit(solution)/shard_map/while/body/eval_jaxpr/scatter-add | solution.py:136
  1202.8 16.3 %scatter_fusion = f32[13313,64]{1,0:T(8,128)} fusion(f32[13313,64]{1,0:T(8,128)} %get-tuple-element.429, s32[1248]{0:T(1024)S(1)} %fusion.78, f32[1248,64]{1,0:T(8,128)S(1)} %bitcast.139), kind=kCustom, calls=%fused_computation.clone.1 | custom fusion | flops 79872 | bytes 963456 | tf_op jit(solution)/shard_map/while/body/eval_jaxpr/scatter-add | solution.py:136
  1260.5 16.3 %scatter_fusion = f32[13313,64]{1,0:T(8,128)} fusion(f32[13313,64]{1,0:T(8,128)} %get-tuple-element.429, s32[1248]{0:T(1024)S(1)} %fusion.78, f32[1248,64]{1,0:T(8,128)S(1)} %bitcast.139), kind=kCustom, calls=%fused_computation.clone.1 | custom fusion | flops 79872 | bytes 963456 | tf_op jit(solution)/shard_map/while/body/eval_jaxpr/scatter-add | solution.py:136
  1279.8 16.3 %scatter_fusion = f32[13313,64]{1,0:T(8,128)} fusion(f32[13313,64]{1,0:T(8,128)} %get-tuple-element.429, s32[1248]{0:T(1024)S(1)} %fusion.78, f32[1248,64]{1,0:T(8,128)S(1)} %bitcast.139), kind=kCustom, calls=%fused_computation.clone.1 | custom fusion | flops 79872 | bytes 963456 | tf_op jit(solution)/shard_map/while/body/eval_jaxpr/scatter-add | solution.py:136
  1299.0 16.3 %scatter_fusion = f32[13313,64]{1,0:T(8,128)} fusion(f32[13313,64]{1,0:T(8,128)} %get-tuple-element.429, s32[1248]{0:T(1024)S(1)} %fusion.78, f32[1248,64]{1,0:T(8,128)S(1)} %bitcast.139), kind=kCustom, calls=%fused_computation.clone.1 | custom fusion | flops 79872 | bytes 963456 | tf_op jit(solution)/shard_map/while/body/eval_jaxpr/scatter-add | solution.py:136
  1356.7 16.3 %scatter_fusion = f32[13313,64]{1,0:T(8,128)} fusion(f32[13313,64]{1,0:T(8,128)} %get-tuple-element.429, s32[1248]{0:T(1024)S(1)} %fusion.78, f32[1248,64]{1,0:T(8,128)S(1)} %bitcast.139), kind=kCustom, calls=%fused_computation.clone.1 | custom fusion | flops 79872 | bytes 963456 | tf_op jit(solution)/shard_map/while/body/eval_jaxpr/scatter-add | solution.py:136
  1412.3 78.3 %all-reduce.3 = (f32[14,7]{0,1:T(8,128)S(1)}, f32[14]{0:T(128)S(1)}, f32[14,19,57]{2,1,0:T(8,128)S(1)}, f32[57]{0:T(128)S(1)}) all-reduce(f32[14,7]{0,1:T(8,128)S(1)} %convolution_bitcast_fusion.2, f32[14]{0:T(128)S(1)} %get-tuple-element.362, ...), channel_id=1, replica_groups=mesh['wide'=64,'rep'=4] {'wide','rep'}, use_global_device_ids=true, to_apply=%region_4.5 | all-reduce | flops 15331 | bytes 122648 | tf_op jit(solution)/shard_map/psum | solution.py:117
  (749 shorter events, 583.9 us)
Async XLA Ops:
  7.2 150.7 %all-gather.2.cloned.1.call-start = ((), (), s32[]{:S(2)}) async-start(), calls=%async_computation.1 | async-start | bytes 5191680 | tf_op jit(solution)/shard_map/all_gather | solution.py:125
  10.4 4.2 copy-start.10
  10.4 4.2 copy-start.14
  14.6 2.5 copy-start.2
  17.1 0.9 copy-start.9
  17.2 0.9 copy-start.15
  17.4 6.0 copy-start
  17.4 6.0 copy-start.1
  17.4 3.7 copy-start.8
  17.4 3.7 copy-start.11
  21.1 2.5 copy-start.6
  22.0 27.4 %copy-start.4 = (f32[8,96,64]{1,2,0:T(8,128)}, f32[8,96,64]{1,2,0:T(8,128)S(1)}, u32[]{:S(2)}) copy-start(f32[8,96,64]{1,2,0:T(8,128)S(1)} %convolution_add_fusion) | copy-start | bytes 589828
  40.4 11.3 copy-start.13
  41.4 62.2 %copy-start.12 = (s32[8,39,4]{1,2,0:T(4,128)S(1)}, s32[8,39,4]{1,2,0:T(4,128)}, u32[]{:S(2)}) copy-start(s32[8,39,4]{1,2,0:T(4,128)} %param.19) | copy-start | bytes 14980
  51.6 1441.3 %reduce-scatter.2.cloned.1.call-start = ((), (), s32[]{:S(2)}) async-start(), calls=%async_computation.2 | async-start | bytes 5242880 | tf_op jit(solution)/shard_map/reduce_scatter | solution.py:142
  157.9 3.1 copy-start.16
  1404.3 0.9 copy-start.5
  1404.3 1.0 copy-start.7
  1405.3 3.8 copy-start.3
Sparse Core Ops, SparseCore 0:
  51.7 83.0 all-gather.1
  1404.4 47.2 reduce-scatter.1
where the time goes:
time: 1520 us; the launch traced here: 1500 us
  other arithmetic  1060 us (70%)
  local copies, waits for them, and re-layouts  209 us (14%)
  blocking collectives  185 us (12%)
  matrix products  30 us (2%)
    scatter-add x64, other arithmetic, add_block(): partial_value.at[target.reshape(-1)]  1040 us
    psum x1, blocking collectives, local(): dense_sums = lax.psum(dense_terms, ('wide', 'rep'))  78.3 us
    dynamic_slice x64, local copies, waits for them, and re-layouts, add_block(): grad_here = lax.dynamic_slice_in_dim(shard_grad, offset, block_rows, 0)  57.1 us
    dynamic_slice x128, local copies, waits for them, and re-layouts, add_block(): ids_here = lax.dynamic_slice_in_dim(group_ids, offset, block_rows, 0)  55.7 us
    all_gather x1, blocking collectives, local(): lax.all_gather(bag_ids, 'wide', axis=0, tiled=True)  54.2 us
    all_gather x1, blocking collectives, local(): lax.all_gather(bag_lengths, 'wide', axis=0, tiled=True)  52 us
    dynamic_slice x64, local copies, waits for them, and re-layouts, add_block(): lax.dynamic_slice_in_dim(group_lengths, offset, block_rows, 0)  43.4 us
  transfers between devices with their start and end apart: 2, of which 0 were waited for; matrix products, arithmetic and copies ran while one was open for 1% of the time, Pallas kernels for 0%

commit v1 on v0

v1 whole, which is shorter than its diff:
```python
import math

import jax
import jax.numpy as jnp
from jax import lax
from jax.experimental import pallas as pl
from jax.experimental.pallas import tpu as pltpu
from jax.sharding import PartitionSpec as P

K = 64
F = 39
NT = 26
C = 14
KH = 7
BAG = 4
B_DEV = 8
T_SHARE = 128
P_SIZE = 19
NF = 57
FT = 96
SAMPLES = 2048
TROWS = 32768
N_WIDE = 64
N_REP = 4

ROWS = C * P_SIZE
RPAD = 272
LANES = B_DEV * K
FPAD = 40
BAGS = B_DEV * FPAD
MSG = 32
SLOT_ROWS = 1280
META = 144
MESH = pl.DeviceIdType.MESH
VMEM_LIMIT = 56 * 1024 * 1024
f32 = jnp.float32
bf16 = jnp.bfloat16
i32 = jnp.int32


def split(x):
    hi = x.astype(bf16)
    return hi, (x - hi.astype(f32)).astype(bf16)


def mm(a, b, contract=((1,), (0,))):
    return lax.dot_general(a, b, (contract, ((), ())), preferred_element_type=f32)


def mm3(a, b, contract=((1,), (0,))):
    return mm(a[0], b[0], contract) + (mm(a[1], b[0], contract) + mm(a[0], b[1], contract))


NT_DIMS = ((1,), (1,))
TN_DIMS = ((0,), (0,))


def iota(shape, dim):
    return lax.broadcasted_iota(i32, shape, dim)


def dense_kernel(cw, cb, emb, cot, gram, rw, rb, ids, send, aux, xs, tz, rws, fs, fg):
    me_x = lax.axis_index("rep")
    me_w = lax.axis_index("wide")
    for m in range(B_DEV // 2):
        pair = jnp.concatenate([emb[2 * m].astype(f32), emb[2 * m + 1].astype(f32)], axis=1)
        xs[0:F, 128 * m : 128 * m + 128] = pair
    xs[F : F + 1, :] = jnp.ones((1, LANES), f32)
    xb = xs[...].astype(bf16)
    p_at = iota((P_SIZE, FPAD), 0)
    j_at = iota((P_SIZE, FPAD), 1)
    bands = [((j_at == 2 * p_at + (m - 3)) & (j_at < F)).astype(f32) for m in range(KH + 1)]
    last = (j_at == F).astype(f32)
    tz[ROWS:RPAD, :] = jnp.zeros((RPAD - ROWS, FPAD), f32)
    tz[RPAD + ROWS :, :] = jnp.zeros((RPAD - ROWS, FPAD), f32)
    rws[...] = jnp.zeros((RPAD, K), f32)
    for c in range(C):
        even = cb[c] * last
        odd = even
        for d in range(KH):
            even = even + cw[c, d] * bands[d]
            odd = odd + cw[c, d] * bands[d + 1]
        tz[c * P_SIZE : (c + 1) * P_SIZE, :] = even
        tz[RPAD + c * P_SIZE : RPAD + (c + 1) * P_SIZE, :] = odd
        rws[c * P_SIZE : (c + 1) * P_SIZE, 0:NF] = rw[c]
    band = tz[...]
    band_s = split(band)
    act = jnp.tanh(mm(band_s[0], xb) + mm(band_s[1], xb))
    act_e = act[:RPAD]
    act_o = act[RPAD:]
    pooled = 0.5 * (act_e + act_o)
    row_at = iota((RPAD, LANES), 0)
    pooled = jnp.where(row_at == ROWS, 1.0, pooled)
    pooled_s = split(pooled)
    rw_only = rws[...]
    rws[ROWS : ROWS + 1, 0:NF] = rb[...]
    rwt_s = split(rws[...].T)
    new_maps = jnp.tanh(mm3(rwt_s, pooled_s))
    fs[0:F, :] = xs[0:F, :]
    fs[F:FT, :] = new_maps[0:NF]
    low = iota((FT, 128), 1) < K
    for m in range(B_DEV // 2):
        pair = fs[:, 128 * m : 128 * m + 128]
        pair_s = jnp.concatenate(split(pair), axis=1)
        halves = []
        for s in (2 * m, 2 * m + 1):
            g = gram[s]
            part = mm(g, pair_s) + mm(g, pair_s, TN_DIMS)
            halves.append(part[:, 0:128] + part[:, 128:256])
        direct = jnp.concatenate([cot[2 * m].astype(f32), cot[2 * m + 1].astype(f32)], axis=1)
        fg[0:FT, 128 * m : 128 * m + 128] = direct + jnp.where(low, halves[0], halves[1])
    fg[FT:, :] = jnp.zeros((8, LANES), f32)
    recg = fg[F : F + K, :] * (1.0 - new_maps * new_maps)
    recg = jnp.where(iota((K, LANES), 0) < NF, recg, 0.0)
    recg_s = split(recg)
    pooled_grad = mm3(split(rw_only), recg_s)
    half = 0.5 * pooled_grad
    conv_grad = jnp.concatenate(
        [half * (1.0 - act_e * act_e), half * (1.0 - act_o * act_o)], axis=0
    )
    cg_s = split(conv_grad)
    emb_grad = fg[0:FPAD, :] + mm3(split(band.T), cg_s)

    low = iota((FPAD, 128), 1) < K
    lows, highs = [], []
    for m in range(B_DEV // 2):
        pair = emb_grad[:, 128 * m : 128 * m + 128]
        other = pltpu.roll(pair, K, 1)
        lows += [jnp.where(low, pair, 0.0), jnp.where(low, other, 0.0)]
        highs += [jnp.where(low, 0.0, other), jnp.where(low, 0.0, pair)]
    bag_rows = jnp.concatenate(lows + highs, axis=0).astype(bf16)

    owner_at = iota((N_WIDE, BAGS), 0)
    values, owners, owned = [], [], []
    count = jnp.zeros((N_WIDE, BAGS), f32)
    for j in range(BAG):
        v = ids[j : j + 1, :]
        w = jnp.where(v >= 0, (v >> 9) & (N_WIDE - 1), -1)
        hit = (owner_at == w).astype(f32)
        values.append(v)
        owners.append(w)
        owned.append(hit)
        count = count + hit
    before = (iota((BAGS, BAGS), 0) < iota((BAGS, BAGS), 1)).astype(f32).astype(bf16)
    ahead = mm(count.astype(bf16), before)
    places = ([], [])
    codes = jnp.zeros((2 * N_WIDE, 128), f32)
    slot_at = iota((128, BAGS), 0)
    tile_at = (me_w & 3) * 4
    for j in range(BAG):
        rank = jnp.sum(owned[j] * ahead, axis=0, keepdims=True).astype(i32)
        ahead = ahead + owned[j]
        v, w = values[j], owners[j]
        late = rank - 32
        row = jnp.where(rank < 32, rank & 15, 16 + tile_at + (late & 3))
        side = jnp.where(rank < 32, rank >> 4, late >> 2)
        at = w * MSG + row
        for h in range(2):
            places[h].append(jnp.where((w >= 0) & (side == h), at, -1))
        first = ((v >> 15) * 4 + ((v >> 7) & 3) + 1).astype(f32)
        second = (v & (T_SHARE - 1)).astype(f32)
        lhs = jnp.concatenate([owned[j] * first, owned[j] * second], axis=0).astype(bf16)
        codes = codes + mm(lhs, (slot_at == rank).astype(f32).astype(bf16), NT_DIMS)
    aux[:, 0, :] = codes[0:N_WIDE] * 128.0 + codes[N_WIDE:]
    group = 8
    for c in range(N_WIDE // group):
        rows_at = iota((group * MSG, BAGS), 0) + c * group * MSG
        picks = []
        for h in range(2):
            hit = rows_at == places[h][0]
            for j in range(1, BAG):
                hit = hit | (rows_at == places[h][j])
            picks.append(hit.astype(f32).astype(bf16))
        rows = mm(jnp.concatenate(picks, axis=1), bag_rows)
        send[c * group : (c + 1) * group] = rows.astype(bf16).reshape(group, MSG, 128)

    rec_term = mm3(pooled_s, recg_s, NT_DIMS)
    cross = mm(cg_s[0], xb, NT_DIMS) + mm(cg_s[1], xb, NT_DIMS)
    row_at = iota((RPAD, FPAD), 0)
    chan = (row_at * 3450) >> 16
    shift = iota((RPAD, FPAD), 1) - 2 * (row_at - chan * P_SIZE) + 3
    inside = iota((RPAD, FPAD), 1) < F
    cross_e, cross_o = cross[:RPAD], cross[RPAD:]
    lane_at = iota((RPAD, 128), 1)
    taps = jnp.where(lane_at == KH, cross_e[:, F : F + 1] + cross_o[:, F : F + 1], 0.0)
    for d in range(KH):
        diag = jnp.where(inside & (shift == d), cross_e, 0.0) + jnp.where(
            inside & (shift == d + 1), cross_o, 0.0
        )
        taps = jnp.where(lane_at == d, jnp.sum(diag, axis=1, keepdims=True), taps)
    chan_at = (iota((16, RPAD), 1) * 3450) >> 16
    pick = (chan_at == iota((16, RPAD), 0)).astype(f32).astype(bf16)
    taps_s = split(taps)
    conv_term = mm(pick, taps_s[0]) + mm(pick, taps_s[1])
    pay = jnp.concatenate([rec_term[0:136], rec_term[136:272]], axis=1)
    aux[:, 1, :] = pay[0:64]
    aux[:, 2, :] = pay[64:128]
    aux[:, 3, :] = jnp.concatenate(
        [pay[128:136], conv_term, jnp.zeros((N_WIDE - 24, 128), f32)], axis=0
    )


def dense(cw, cb, emb, cot, gram, rw, rb, ids):
    smem = pl.BlockSpec(memory_space=pltpu.SMEM)
    vmem = pl.BlockSpec(memory_space=pltpu.VMEM)
    return pl.pallas_call(
        dense_kernel,
        out_shape=(
            jax.ShapeDtypeStruct((N_WIDE, MSG, 128), bf16),
            jax.ShapeDtypeStruct((N_WIDE, 4, 128), f32),
        ),
        in_specs=[smem, smem, vmem, vmem, vmem, vmem, vmem, vmem],
        out_specs=(vmem, vmem),
        scratch_shapes=[
            pltpu.VMEM((FPAD, LANES), f32),
            pltpu.VMEM((2 * RPAD, FPAD), f32),
            pltpu.VMEM((RPAD, K), f32),
            pltpu.VMEM((FT, LANES), f32),
            pltpu.VMEM((FT + 8, LANES), f32),
        ],
        compiler_params=pltpu.CompilerParams(vmem_limit_bytes=VMEM_LIMIT),
        name="dense_pack",
    )(cw, cb, emb, cot, gram, rw, rb, ids)


def exchange_kernel(send, aux, vt, red, rdat, raux, part, parts, sems):
    me_w = lax.axis_index("wide")
    me_x = lax.axis_index("rep")

    def peer(o):
        return lax.rem(me_w + o, N_WIDE)

    def wide_copy(src, dst, to, s, r):
        return pltpu.make_async_remote_copy(
            src_ref=src, dst_ref=dst, send_sem=sems.at[s], recv_sem=sems.at[r],
            device_id=(to, me_x), device_id_type=MESH,
        )

    def rep_copy(src, dst, o, s, r):
        return pltpu.make_async_remote_copy(
            src_ref=src, dst_ref=dst, send_sem=sems.at[s], recv_sem=sems.at[r],
            device_id=(me_w, lax.rem(me_x + o, N_REP)), device_id_type=MESH,
        )

    def wait_bytes(ref, n, s):
        pltpu.make_async_copy(ref.at[pl.ds(0, n)], ref.at[pl.ds(0, n)], sems.at[s]).wait()

    barrier = pltpu.get_barrier_semaphore()

    def greet(o, carry):
        pl.semaphore_signal(barrier, inc=1, device_id=(peer(o), me_x), device_id_type=MESH)
        return carry

    lax.fori_loop(1, N_WIDE, greet, 0)
    for o in range(1, N_REP):
        pl.semaphore_signal(
            barrier, inc=1, device_id=(me_w, lax.rem(me_x + o, N_REP)), device_id_type=MESH
        )
    pl.semaphore_wait(barrier, N_WIDE - 1 + N_REP - 1)

    def start_all(o, carry):
        to = peer(o)
        wide_copy(aux.at[to], raux.at[me_w], to, 0, 1).start()
        wide_copy(send.at[to], rdat.at[me_w], to, 2, 3).start()
        return carry

    lax.fori_loop(1, N_WIDE, start_all, 0)
    raux[me_w] = aux[me_w]
    rdat[me_w] = send[me_w]

    wait_bytes(raux, N_WIDE - 1, 1)
    part[...] = jnp.sum(raux[...], axis=0)
    for o in range(1, N_REP):
        rep_copy(part, parts.at[me_x], o, 4, 5).start()
    parts[me_x] = part[...]

    codes = raux[:, 0, :]
    lane = iota((N_WIDE, 128), 1)
    src = iota((N_WIDE, 128), 0)
    flat = []
    for h in range(2):
        near = pltpu.roll(codes, 128 - 16 * h, 1) if h else codes
        near = jnp.where(lane < 16, near, 0.0)
        for by in (16, 32, 64):
            near = near + pltpu.roll(near, by, 1)
        near = jnp.where((lane >> 4) == (src & 7), near, 0.0)
        near = jnp.sum(near.reshape(8, 8, 128), axis=1)
        late = pltpu.roll(codes, 128 - 32 - 4 * h, 1)
        late = jnp.where(lane < 4, late, 0.0)
        for by in (4, 8, 16, 32, 64):
            late = late + pltpu.roll(late, by, 1)
        late = jnp.where((lane >> 2) == (src & 31), late, 0.0)
        late = jnp.sum(late.reshape(2, 32, 128), axis=1)
        flat.append(jnp.concatenate([near, late], axis=0))
    high = [jnp.floor(x * (1.0 / 128.0)) for x in flat]
    small = [x - 128.0 * y for x, y in zip(flat, high)]
    meta_at = iota((16, 128), 0)
    for g in range(10):
        rows = jnp.zeros((16, 128), f32)
        for n, x in enumerate((high[0], small[0], high[1], small[1])):
            rows = jnp.where(meta_at == n, x[g : g + 1, :], rows)
        vt[me_x, 128:META, 128 * g : 128 * g + 128] = rows.astype(bf16)

    wait_bytes(rdat, N_WIDE - 1, 3)
    for g in range(8):
        rows = rdat[8 * g : 8 * g + 8, 0:16, :].reshape(128, 128).astype(f32)
        vt[me_x, 0:128, 128 * g : 128 * g + 128] = rows.T.astype(bf16)
    for e in range(2):
        rows = rdat[32 * e : 32 * e + 32, 16:32, :].astype(f32)
        rows = jnp.sum(rows.reshape(8, 4, 16, 128), axis=1).reshape(128, 128)
        vt[me_x, 0:128, 1024 + 128 * e : 1024 + 128 * e + 128] = rows.T.astype(bf16)
    for o in range(1, N_REP):
        rep_copy(vt.at[me_x], vt.at[me_x], o, 6, 7).start()

    wait_bytes(parts, N_REP - 1, 5)
    red[me_w] = (parts[0] + parts[1]) + (parts[2] + parts[3])

    def start_sums(o, carry):
        wide_copy(red.at[me_w], red.at[me_w], peer(o), 8, 9).start()
        return carry

    lax.fori_loop(1, N_WIDE, start_sums, 0)
    wait_bytes(red, N_WIDE - 1, 9)
    wait_bytes(red, N_WIDE - 1, 8)
    wait_bytes(raux, N_WIDE - 1, 0)
    wait_bytes(rdat, N_WIDE - 1, 2)
    wait_bytes(parts, N_REP - 1, 4)
    wait_bytes(vt, N_REP - 1, 7)
    wait_bytes(vt, N_REP - 1, 6)


def exchange(send, aux):
    vmem = pl.BlockSpec(memory_space=pltpu.VMEM)
    return pl.pallas_call(
        exchange_kernel,
        out_shape=(
            jax.ShapeDtypeStruct((N_REP, META, SLOT_ROWS), bf16),
            jax.ShapeDtypeStruct((N_WIDE, 4, 128), f32),
        ),
        in_specs=[vmem, vmem],
        out_specs=(vmem, vmem),
        scratch_shapes=[
            pltpu.VMEM((N_WIDE, MSG, 128), bf16),
            pltpu.VMEM((N_WIDE, 4, 128), f32),
            pltpu.VMEM((4, 128), f32),
            pltpu.VMEM((N_REP, 4, 128), f32),
            pltpu.SemaphoreType.DMA((10,)),
        ],
        compiler_params=pltpu.CompilerParams(
            vmem_limit_bytes=VMEM_LIMIT, collective_id=0, has_side_effects=True
        ),
        name="exchange",
    )(send, aux)


def gather_kernel(scale, vt, red, table, conv_w, conv_b, rec_w, rec_b, acc, pays, wide_w):
    me_x = lax.axis_index("rep")
    row_at = iota((256, SLOT_ROWS), 0)
    for x in range(N_REP):
        for h in range(2):
            rows = vt[x, K * h : K * h + K, :]
            meta = vt[x, 128:META, :].astype(f32).astype(i32)
            code = meta[2 * h : 2 * h + 1, :] - 1
            table_at = code >> 2
            mine = (code >= 0) & ((code & 3) == me_x)
            target = jnp.where(
                mine, (table_at & 1) * T_SHARE + meta[2 * h + 1 : 2 * h + 2, :], -1
            )
            hits = (row_at == target).astype(f32).astype(bf16)
            pair_at = table_at >> 1
            spread = jnp.concatenate(
                [rows * (pair_at == t).astype(f32).astype(bf16) for t in range(NT // 2)], axis=0
            )
            term = mm(spread, hits, NT_DIMS)
            if x == 0 and h == 0:
                acc[...] = term
            else:
                acc[...] += term
    for t in range(NT):
        half = (t % 2) * T_SHARE
        table[t] = acc[(t // 2) * K : (t // 2) * K + K, half : half + T_SHARE]

    for g in range(3):
        pays[64 * g : 64 * g + 64, :] = red[:, 1 + g, :] * scale
    wide_w[0:136, :] = pays[0:136, :]
    wide_w[136:272, :] = pltpu.roll(pays[0:136, :], K, 1)
    for c in range(C):
        rec_w[c] = wide_w[c * P_SIZE : (c + 1) * P_SIZE, 0:NF]
    rec_b[...] = wide_w[ROWS : ROWS + 1, 0:NF]
    conv = pays[136:152, :]
    conv_w[...] = conv[0:C, 0:KH]
    square = iota((16, 128), 0) == iota((16, 128), 1)
    bias = jnp.sum(jnp.where(square, conv[:, KH : KH + 1], 0.0), axis=0, keepdims=True)
    conv_b[...] = bias[:, 0:C]


def gather(scale, vt, red):
    vmem = pl.BlockSpec(memory_space=pltpu.VMEM)

    def kernel(*refs):
        gather_kernel(scale, *refs)

    return pl.pallas_call(
        kernel,
        out_shape=(
            jax.ShapeDtypeStruct((NT, K, T_SHARE), f32),
            jax.ShapeDtypeStruct((C, KH), f32),
            jax.ShapeDtypeStruct((1, C), f32),
            jax.ShapeDtypeStruct((C, P_SIZE, NF), f32),
            jax.ShapeDtypeStruct((1, NF), f32),
        ),
        in_specs=[vmem, vmem],
        out_specs=(vmem,) * 5,
        scratch_shapes=[
            pltpu.VMEM((NT // 2 * K, 256), f32),
            pltpu.VMEM((192, 128), f32),
            pltpu.VMEM((RPAD, 128), f32),
        ],
        compiler_params=pltpu.CompilerParams(vmem_limit_bytes=VMEM_LIMIT),
        name="table_rows",
    )(vt, red)


def slot_values(bag_ids, bag_lengths, field_table):
    live = jnp.arange(BAG, dtype=i32)[None, None, :] < bag_lengths[:, :, None]
    value = jnp.where(live, field_table[None, :, None] * TROWS + bag_ids, -1)
    value = jnp.pad(value, ((0, 0), (0, FPAD - F), (0, 0)), constant_values=-1)
    return value.transpose(2, 0, 1).reshape(BAG, BAGS)


def local(
    pooled_emb, conv_weight, conv_bias, rec_weight, rec_bias, feat_cot, gram_cot, bag_ids,
    bag_lengths, field_table,
):
    ids = slot_values(bag_ids, bag_lengths, field_table)
    send, aux = dense(
        conv_weight, conv_bias, pooled_emb, feat_cot, gram_cot, rec_weight,
        rec_bias.reshape(1, NF), ids,
    )
    vt, red = exchange(send, aux)
    table, conv_w, conv_b, rec_w, rec_b = gather(1.0 / math.sqrt(SAMPLES), vt, red)
    return table, conv_w, conv_b.reshape(C), rec_w, rec_b.reshape(NF)


def solution(mesh):
    in_specs = (
        P(("wide", "rep"), None, None), P(), P(), P(), P(), P(("wide", "rep"), None, None),
        P(("wide", "rep"), None, None), P(("wide", "rep"), None, None), P(("wide", "rep"), None),
        P(),
    )
    out_specs = (P(None, None, ("wide", "rep")), P(), P(), P(), P())
    return jax.shard_map(local, mesh=mesh, in_specs=in_specs, out_specs=out_specs, check_vma=False)
```

time: 1520 us -> 76.9 us (0.05); the launches traced: 1500 us -> 76.6 us
  other arithmetic: 1060 us -> 1.38 us
  local copies, waits for them, and re-layouts: 209 us -> 9.87 us
  blocking collectives: 185 us -> 0 us
  Pallas kernels: 0 us -> 64.6 us
  matrix products: 30 us -> 0 us
    scatter-add x64 -> x0, other arithmetic: 1040 us -> none  [add_block(): partial_value.at[target.reshape(-1)]]
    dynamic_slice x256 -> x0, local copies, waits for them, and re-layouts: 156 us -> none  [the longest x64 57.1 us: add_block(): grad_here = lax.dynamic_slice_in_dim(shard_grad, offset, block_rows, 0)]
    all_gather x2 -> x0, blocking collectives: 106 us -> none  [the longest x1 54.2 us: local(): lax.all_gather(bag_ids, 'wide', axis=0, tiled=True)]
    psum x1 -> x0, blocking collectives: 78.3 us -> none  [local(): dense_sums = lax.psum(dense_terms, ('wide', 'rep'))]
    pallas_call x0 -> x3, Pallas kernels: none -> 64.6 us  [the longest x1 49.4 us: exchange(): pl.pallas_call(exchange_kernel, out_shape=(jax.ShapeDtypeStruct((N_REP, M...]
    dot_general x13 -> x0, matrix products: 30 us -> none  [the longest x7 15.7 us: dense_backward(): jnp.einsum('c,bcik->bik', conv_weight[:, shift], window, precision=highest)]
  transfers between devices with their start and end apart: 2 -> 0, of which waited for: 0 -> 0; matrix products, arithmetic and copies ran while one was open for 1% -> 0% of each run, Pallas kernels for 0% -> 0%
where the time goes in v1:
time: 76.9 us; the launch traced here: 76.6 us
  Pallas kernels  64.6 us (84%)
  local copies, waits for them, and re-layouts  9.87 us (13%)
  other arithmetic  1.38 us (2%)
    pallas_call x1, Pallas kernels, exchange(): pl.pallas_call(exchange_kernel, out_shape=(jax.ShapeDtypeStruct((N_REP, M...  49.4 us
    unnamed x6, local copies, waits for them, and re-layouts  9.19 us
    pallas_call x1, Pallas kernels, dense(): pl.pallas_call(dense_kernel, out_shape=(jax.ShapeDtypeStruct((N_WIDE, MSG...  8.22 us
    pallas_call x1, Pallas kernels, gather(): pl.pallas_call(kernel, out_shape=(jax.ShapeDtypeStruct((NT, K, T_SHARE),...  6.98 us

profile of v1, /device:TPU:1, one launch (start us, length us, event | category | flops | bytes accessed | tf_op | source)
XLA Modules:
  0.0 76.6 jit_solution(7956634934503369526)
XLA Ops:
  0.6 0.7 broadcast_multiply_fusion
  1.3 1.4 %copy.16.cw = f32[14,7]{1,0:T(8,128)} copy(f32[14,7]{0,1:T(8,128)} %param.11) | data formatting | bytes 784 | tf_op args[1]
  2.6 0.7 add_select_fusion
  3.4 0.7 reshape.26.ids
  4.1 1.5 %copy.17.emb = bf16[8,39,64]{2,1,0:T(8,128)(2,1)} copy(bf16[8,39,64]{2,0,1:T(8,128)(2,1)} %param.10) | data formatting | bytes 79872 | tf_op args[0]
  5.6 1.6 %copy.19.rw = f32[14,19,57]{2,1,0:T(8,128)} copy(f32[14,19,57]{2,0,1:T(8,128)} %param.13) | data formatting | bytes 121296 | tf_op args[3]
  7.2 1.7 %copy.18.cot = bf16[8,96,64]{2,1,0:T(8,128)(2,1)} copy(bf16[8,96,64]{1,2,0:T(8,128)(2,1)} %param.15) | data formatting | bytes 196608 | tf_op args[5]
  8.9 8.2 %dense_pack.1 = (bf16[64,32,128]{2,1,0:T(8,128)(2,1)}, f32[64,4,128]{2,1,0:T(4,128)}) custom-call(f32[14,7]{1,0:T(8,128)} %copy.16.cw, f32[14]{0:T(128)} %cb.1, bf16[8,39,64]{2,1,0:T(8,128)(2,1)} %copy.17.emb, bf16[8,96,64]{2,1,0:T(8,128)(2,1)} %copy.18.cot, bf16[8,96,96]{2,1,0:T(8,128)(2,1)} %gram.1, f32[14,19,57]{2,1,0:T(8,128)} %copy.19.rw, ...), custom_call_target="tpu_custom_call" | custom-call | tf_op jit(solution)/shard_map/dense_pack/pallas_call | solution.py:206
  17.1 49.4 %exchange.1 = (bf16[4,144,1280]{2,1,0:T(8,128)(2,1)}, f32[64,4,128]{2,1,0:T(4,128)}) custom-call(bf16[64,32,128]{2,1,0:T(8,128)(2,1)} %get-tuple-element.14.send, f32[64,4,128]{2,1,0:T(4,128)} %get-tuple-element.15.aux), custom_call_target="tpu_custom_call" | custom-call | tf_op jit(solution)/shard_map/exchange/pallas_call | solution.py:334
  66.6 7.0 %table_rows.1 = (f32[26,64,128]{2,1,0:T(8,128)}, f32[14,7]{1,0:T(8,128)}, f32[1,14]{1,0:T(1,128)}, f32[14,19,57]{2,1,0:T(8,128)}, f32[1,57]{1,0:T(1,128)}) custom-call(bf16[4,144,1280]{2,1,0:T(8,128)(2,1)} %get-tuple-element.16.refs_0_, f32[64,4,128]{2,1,0:T(4,128)} %get-tuple-element.17.refs_1_), custom_call_target="tpu_custom_call" | custom-call | tf_op jit(solution)/shard_map/table_rows/pallas_call | solution.py:403
  73.6 1.4 %copy.20 = f32[14,7]{0,1:T(8,128)} copy(f32[14,7]{1,0:T(8,128)} %get-tuple-element.24) | data formatting | bytes 784
  74.9 1.6 %copy.21 = f32[14,19,57]{2,0,1:T(8,128)} copy(f32[14,19,57]{2,1,0:T(8,128)} %get-tuple-element.26) | data formatting | bytes 121296
  (2 shorter events, 0.0 us)

commit v2 on v0

v2 whole, which is shorter than its diff:
```python
import math

import jax
import jax.numpy as jnp
from jax import lax
from jax.experimental import pallas as pl
from jax.experimental.pallas import tpu as pltpu
from jax.sharding import PartitionSpec as P

K = 64
F = 39
NT = 26
C = 14
KH = 7
BAG = 4
B_DEV = 8
T_SHARE = 128
P_SIZE = 19
NF = 57
FT = 96
SAMPLES = 2048
TROWS = 32768
N_WIDE = 64
N_REP = 4

ROWS = C * P_SIZE
RPAD = 272
LANES = B_DEV * K
FPAD = 40
BAGS = B_DEV * FPAD
MSG = 24
GROUPS = 4
CHUNKS = GROUPS + 1
BLOCK = 72
MESH = pl.DeviceIdType.MESH
VMEM_LIMIT = 56 * 1024 * 1024
f32 = jnp.float32
bf16 = jnp.bfloat16
i32 = jnp.int32


def split(x):
    hi = x.astype(bf16)
    return hi, (x - hi.astype(f32)).astype(bf16)


def mm(a, b, contract=((1,), (0,))):
    return lax.dot_general(a, b, (contract, ((), ())), preferred_element_type=f32)


def mm3(a, b, contract=((1,), (0,))):
    return mm(a[0], b[0], contract) + (mm(a[1], b[0], contract) + mm(a[0], b[1], contract))


NT_DIMS = ((1,), (1,))
TN_DIMS = ((0,), (0,))


def iota(shape, dim):
    return lax.broadcasted_iota(i32, shape, dim)


def dense_part(
    me_w, cw, cb, emb, cot, gram, rw, rb, ids, lengths, field_table,
    send, stage, es, xs, tz, rws, fs, fg, ip,
):
    es[:, 0:K] = emb[...].astype(f32).reshape(F * B_DEV, K)
    for m in range(B_DEV // 2):
        pair = [es[pl.ds(2 * m + e, F, stride=B_DEV), :][:, 0:K] for e in range(2)]
        xs[0:F, 128 * m : 128 * m + 128] = jnp.concatenate(pair, axis=1)
    xs[F : F + 1, :] = jnp.ones((1, LANES), f32)
    xb = xs[...].astype(bf16)
    taps = jnp.concatenate([cw[...], cb[...]], axis=0).T
    taps = jnp.concatenate([taps, jnp.zeros((C, 120), f32)], axis=1)
    lane = iota((C, 128), 1)
    kernel_taps = jnp.where(lane < KH, taps, 0.0)
    bias_tap = pltpu.roll(jnp.where(lane == KH, taps, 0.0), F - KH, 1)
    tz[ROWS:RPAD, :] = jnp.zeros((RPAD - ROWS, 128), f32)
    tz[RPAD + ROWS :, :] = jnp.zeros((RPAD - ROWS, 128), f32)
    rws[...] = jnp.zeros((RPAD, K), f32)
    for p in range(P_SIZE):
        for odd in range(2):
            moved = pltpu.roll(kernel_taps, (2 * p + odd - 3) % 128, 1)
            rows = pl.ds(odd * RPAD + p * C, C)
            tz[rows, :] = jnp.where(lane < F, moved, 0.0) + bias_tap
        rws[p * C : (p + 1) * C, 0:NF] = rw[p]
    band = tz[:, 0:FPAD]
    band_s = split(band)
    act = jnp.tanh(mm(band_s[0], xb) + mm(band_s[1], xb))
    act_e = act[:RPAD]
    act_o = act[RPAD:]
    pooled = 0.5 * (act_e + act_o)
    pooled = jnp.where(iota((RPAD, LANES), 0) == ROWS, 1.0, pooled)
    pooled_s = split(pooled)
    rw_only = rws[...]
    rws[ROWS : ROWS + 1, 0:NF] = rb[...]
    rwt_s = split(rws[...].T)
    new_maps = jnp.tanh(mm3(rwt_s, pooled_s))
    fs[0:F, :] = xs[0:F, :]
    fs[F:FT, :] = new_maps[0:NF]
    fg[0:FT, :] = cot[...].astype(f32).reshape(LANES, FT).T
    low = iota((FT, 128), 1) < K
    for m in range(B_DEV // 2):
        pair_s = jnp.concatenate(split(fs[:, 128 * m : 128 * m + 128]), axis=1)
        halves = []
        for s in (2 * m, 2 * m + 1):
            g = gram[s]
            part = mm(g, pair_s) + mm(g, pair_s, TN_DIMS)
            halves.append(part[:, 0:128] + part[:, 128:256])
        fg[0:FT, 128 * m : 128 * m + 128] += jnp.where(low, halves[0], halves[1])
    fg[FT:, :] = jnp.zeros((8, LANES), f32)
    recg = fg[F : F + K, :] * (1.0 - new_maps * new_maps)
    recg = jnp.where(iota((K, LANES), 0) < NF, recg, 0.0)
    recg_s = split(recg)
    half = 0.5 * mm3(split(rw_only), recg_s)
    conv_grad = jnp.concatenate(
        [half * (1.0 - act_e * act_e), half * (1.0 - act_o * act_o)], axis=0
    )
    cg_s = split(conv_grad)
    emb_grad = fg[0:FPAD, :] + mm3(split(band.T), cg_s)

    low = iota((FPAD, 128), 1) < K
    lows, highs = [], []
    for m in range(B_DEV // 2):
        pair = emb_grad[:, 128 * m : 128 * m + 128]
        other = pltpu.roll(pair, K, 1)
        lows += [jnp.where(low, pair, 0.0), jnp.where(low, other, 0.0)]
        highs += [jnp.where(low, 0.0, other), jnp.where(low, 0.0, pair)]
    bag_rows = jnp.concatenate(lows + highs, axis=0).astype(bf16)

    ip[...] = jnp.zeros((B_DEV, 8, 128), i32)
    slot_at = iota((BAG, F), 0)
    for s in range(B_DEV):
        live = slot_at < lengths[s : s + 1, :]
        ip[s, 0:BAG, 0:F] = jnp.where(live, field_table[...] * TROWS + ids[s] + 1, 0)
    value = jnp.zeros((8, 384), i32)
    for s in range(B_DEV):
        wide = jnp.concatenate([ip[s], jnp.zeros((8, 256), i32)], axis=1)
        value = value + (pltpu.roll(wide, FPAD * s, 1) if s else wide)
    value = value[:, 0:BAGS] - 1

    peer_at = iota((N_WIDE, BAGS), 0)
    values, offsets, owned = [], [], []
    count = jnp.zeros((N_WIDE, BAGS), f32)
    for j in range(BAG):
        v = value[j : j + 1, :]
        o = jnp.where(v >= 0, ((v >> 9) - me_w) & (N_WIDE - 1), -1)
        hit = (peer_at == o).astype(f32)
        values.append(v)
        offsets.append(o)
        owned.append(hit)
        count = count + hit
    before = (iota((BAGS, BAGS), 0) < iota((BAGS, BAGS), 1)).astype(f32).astype(bf16)
    ahead = mm(count.astype(bf16), before)
    near, late = [], []
    codes = jnp.zeros((2 * N_WIDE, 128), f32)
    slot_at = iota((128, BAGS), 0)
    for j in range(BAG):
        rank = jnp.sum(owned[j] * ahead, axis=0, keepdims=True).astype(i32)
        ahead = ahead + owned[j]
        v, o = values[j], offsets[j]
        early = (o >= 0) & (rank < 32)
        after = (o >= 0) & (rank >= 32)
        rest = rank - 32
        near.append(jnp.concatenate(
            [jnp.where(early & ((rank >> 4) == h), o * 16 + (rank & 15), -1) for h in range(2)], axis=1
        ))
        late.append(jnp.concatenate(
            [jnp.where(after & ((rest >> 2) == h), o * 4 + (rest & 3), -1) for h in range(2)], axis=1
        ))
        first = ((v >> 15) * 4 + ((v >> 7) & 3) + 1).astype(f32)
        second = (v & (T_SHARE - 1)).astype(f32)
        lhs = jnp.concatenate([owned[j] * first, owned[j] * second], axis=0).astype(bf16)
        codes = codes + mm(lhs, (slot_at == rank).astype(f32).astype(bf16), NT_DIMS)

    def pick(rows_at, places):
        hit = rows_at == places[0]
        for j in range(1, BAG):
            hit = hit | (rows_at == places[j])
        return mm(hit.astype(f32).astype(bf16), bag_rows)

    stage[...] = jnp.zeros((N_WIDE, 8, 128), f32)
    stage[:, 0:4, :] = pick(iota((256, 2 * BAGS), 0), late).reshape(N_WIDE, 4, 128)
    stage[:, 4, :] = codes[0:N_WIDE] + pltpu.roll(codes[N_WIDE:], K, 1)
    send[:, 16:24, :] = stage[...].astype(bf16)
    for c in range(GROUPS):
        rows = pick(iota((256, 2 * BAGS), 0) + 256 * c, near)
        send[16 * c : 16 * c + 16, 0:16, :] = rows.astype(bf16).reshape(16, 16, 128)
    return xb, pooled_s, recg_s, cg_s


def weight_part(xb, pooled_s, recg_s, cg_s, aux, tz):
    rec_term = mm3(pooled_s, recg_s, NT_DIMS)
    cross = mm(cg_s[0], xb, NT_DIMS) + mm(cg_s[1], xb, NT_DIMS)
    tz[:, 0:FPAD] = cross
    lane = iota((C, 128), 1)
    taps = jnp.zeros((C, 128), f32)
    bias = jnp.zeros((C, 128), f32)
    for p in range(P_SIZE):
        for odd in range(2):
            rows = tz[pl.ds(odd * RPAD + p * C, C), :]
            bias = bias + rows
            taps = taps + pltpu.roll(jnp.where(lane < F, rows, 0.0), (3 - 2 * p - odd) % 128, 1)
    bias = pltpu.roll(jnp.where(lane == F, bias, 0.0), 128 - F + KH, 1)
    taps = jnp.where(lane < KH, taps, 0.0) + bias
    taps = jnp.concatenate([taps, jnp.zeros((128 - C, 128), f32)], axis=0).T[0:8]
    pay = jnp.concatenate([rec_term[0:136], rec_term[136:272]], axis=1)
    aux[:, 0, :] = pay[0:64]
    aux[:, 1, :] = pay[64:128]
    aux[:, 2, :] = jnp.concatenate(
        [pay[128:136], taps, jnp.zeros((N_WIDE - 16, 128), f32)], axis=0
    )


def windows(codes, first, width):
    n = codes.shape[0]
    lane = iota((n, 128), 1)
    src = iota((n, 128), 0)
    out = pltpu.roll(codes, (128 - first) % 128, 1) if first % 128 else codes
    out = jnp.where(lane < width, out, 0.0)
    by = width
    while by < 128:
        out = out + pltpu.roll(out, by, 1)
        by *= 2
    per = 128 // width
    out = jnp.where(lane // width == (src & (per - 1)), out, 0.0)
    out = jnp.sum(out.reshape(n // per, per, 128), axis=1)
    return jnp.concatenate([out[g : g + 1] for g in range(n // per)], axis=1)


def fill_chunk(vt, g, rows, codes, starts, width):
    turned = rows.T
    row_at = iota((8, 256), 0)
    for h in range(2):
        first = windows(codes, starts[h], width)
        second = windows(codes, 64 + starts[h], width)
        meta = jnp.where(row_at == 0, first, jnp.where(row_at == 1, second, 0.0))
        vt[0, g, h] = jnp.concatenate([turned[K * h : K * h + K], meta], axis=0).astype(bf16)


def add_rows(me_x, vt, acc, slot, g):
    meta = [vt[slot, g, h][K:BLOCK].astype(f32) for h in range(2)]
    rows = jnp.concatenate([vt[slot, g, h][0:K] for h in range(2)], axis=1)
    code = jnp.concatenate([m[0:1] for m in meta], axis=1).astype(i32) - 1
    place = jnp.concatenate([m[1:2] for m in meta], axis=1).astype(i32)
    table_at = code >> 2
    mine = (code >= 0) & ((code & 3) == me_x)
    target = jnp.where(mine, (table_at & 1) * T_SHARE + place, -1)
    hits = (iota((256, 512), 0) == target).astype(f32).astype(bf16)
    pair_at = table_at >> 1
    spread = jnp.concatenate(
        [rows * (pair_at == t).astype(f32).astype(bf16) for t in range(NT // 2)], axis=0
    )
    acc[...] += mm(spread, hits, NT_DIMS)


def whole_kernel(
    cw, cb, emb, cot, gram, rw, rb, ids, lengths, field_table,
    table, conv_w, conv_b, rec_w, rec_b,
    send, stage, es, xs, tz, rws, fs, fg, ip, aux,
    rdat, raux, part, parts, red, vt, acc, pays, wide_w,
    data_sems, ring_recv, ring_send, sems,
):
    me_w = lax.axis_index("wide")
    me_x = lax.axis_index("rep")
    right = lax.rem(me_x + 1, N_REP)
    left = lax.rem(me_x + N_REP - 1, N_REP)

    def peer(o):
        return lax.rem(me_w + o, N_WIDE)

    def wide_copy(src, dst, to, s, r):
        return pltpu.make_async_remote_copy(
            src_ref=src, dst_ref=dst, send_sem=s, recv_sem=r,
            device_id=(to, me_x), device_id_type=MESH,
        )

    def rep_copy(src, dst, to, s, r):
        return pltpu.make_async_remote_copy(
            src_ref=src, dst_ref=dst, send_sem=s, recv_sem=r,
            device_id=(me_w, to), device_id_type=MESH,
        )

    def wait_bytes(ref, n, sem):
        pltpu.make_async_copy(ref.at[pl.ds(0, n)], ref.at[pl.ds(0, n)], sem).wait()

    barrier = pltpu.get_barrier_semaphore()

    def greet(o, carry):
        pl.semaphore_signal(barrier, inc=1, device_id=(peer(o), me_x), device_id_type=MESH)
        return carry

    lax.fori_loop(1, N_WIDE, greet, 0)
    for o in range(1, N_REP):
        pl.semaphore_signal(
            barrier, inc=1, device_id=(me_w, lax.rem(me_x + o, N_REP)), device_id_type=MESH
        )

    terms = dense_part(
        me_w, cw, cb, emb, cot, gram, rw, rb, ids, lengths, field_table,
        send, stage, es, xs, tz, rws, fs, fg, ip,
    )
    pl.semaphore_wait(barrier, N_WIDE - 1 + N_REP - 1)

    def send_rows(o, carry):
        wide_copy(
            send.at[o], rdat.at[o], peer(o), sems.at[0], data_sems.at[o // 16]
        ).start()
        return carry

    def send_terms(o, carry):
        to = peer(o)
        wide_copy(aux.at[to], raux.at[me_w], to, sems.at[1], sems.at[2]).start()
        return carry

    def send_sums(o, carry):
        wide_copy(red.at[me_w], red.at[me_w], peer(o), sems.at[5], sems.at[6]).start()
        return carry

    lax.fori_loop(1, SPLIT_AT, send_rows, 0)
    weight_part(*terms, aux, tz)
    lax.fori_loop(1, N_WIDE, send_terms, 0)
    lax.fori_loop(SPLIT_AT, N_WIDE, send_rows, 0)
    rdat[0] = send[0]
    raux[me_w] = aux[me_w]
    acc[...] = jnp.zeros(acc.shape, f32)

    def ring(kind, g):
        slot, h, to, there = (
            (0, 0, right, 1), (0, 1, right, 1), (0, 1, left, 2), (0, 0, left, 2),
            (1, 0, right, 3), (2, 1, left, 3),
        )[kind]
        return rep_copy(
            vt.at[slot, g, h], vt.at[there, g, h], to, ring_send.at[kind], ring_recv.at[kind, g]
        )

    def step(g, carry):
        @pl.when(g < GROUPS)
        def _():
            @pl.when(g == 0)
            def _():
                wait_bytes(rdat, 15, data_sems.at[0])

            @pl.when(g > 0)
            def _():
                wait_bytes(rdat, 16, data_sems.at[g])

            got = rdat[pl.ds(16 * g, 16)]
            rows = got[:, 0:16, :].reshape(256, 128).astype(f32)
            codes = got[:, 16:24, :].astype(f32)[:, 4, :]
            fill_chunk(vt, g, rows, codes, (0, 16), 16)

        @pl.when(g == GROUPS)
        def _():
            tail = rdat[:, 16:24, :].astype(f32)
            rows = tail[:, 0:4, :].reshape(256, 128)
            fill_chunk(vt, GROUPS, rows, tail[:, 4, :], (32, 36), 4)

        @pl.when(g < CHUNKS)
        def _():
            for kind in (0, 2, 1, 3):
                ring(kind, g).start()

        @pl.when((g >= 1) & (g <= CHUNKS))
        def _():
            ring(0, g - 1).wait_recv()
            ring(4, g - 1).start()
            ring(2, g - 1).wait_recv()
            ring(5, g - 1).start()

        @pl.when(g < CHUNKS)
        def _():
            add_rows(me_x, vt, acc, 0, g)

        @pl.when(g == 2)
        def _():
            wait_bytes(raux, N_WIDE - 1, sems.at[2])
            part[...] = jnp.sum(raux[...], axis=0)
            for o in range(1, N_REP):
                to = lax.rem(me_x + o, N_REP)
                rep_copy(part, parts.at[me_x], to, sems.at[3], sems.at[4]).start()
            parts[me_x] = part[...]

        @pl.when((g >= 1) & (g <= CHUNKS))
        def _():
            ring(1, g - 1).wait_recv()
            ring(3, g - 1).wait_recv()
            add_rows(me_x, vt, acc, 1, g - 1)
            add_rows(me_x, vt, acc, 2, g - 1)

        @pl.when(g == 2)
        def _():
            wait_bytes(parts, N_REP - 1, sems.at[4])
            red[me_w] = (parts[0] + parts[1]) + (parts[2] + parts[3])
            lax.fori_loop(1, N_WIDE, send_sums, 0)

        @pl.when(g >= 2)
        def _():
            ring(4, g - 2).wait_recv()
            ring(5, g - 2).wait_recv()
            add_rows(me_x, vt, acc, 3, g - 2)

        return carry

    lax.fori_loop(0, CHUNKS + 2, step, 0)

    for t in range(NT):
        half = (t % 2) * T_SHARE
        table[t] = acc[(t // 2) * K : (t // 2) * K + K, half : half + T_SHARE]

    wait_bytes(red, N_WIDE - 1, sems.at[6])
    scale = 1.0 / math.sqrt(SAMPLES)
    for g in range(3):
        pays[64 * g : 64 * g + 64, :] = red[:, g, :] * scale
    wide_w[0:136, :] = pays[0:136, :]
    wide_w[136:272, :] = pltpu.roll(pays[0:136, :], K, 1)
    for p in range(P_SIZE):
        rec_w[p] = wide_w[p * C : (p + 1) * C, 0:NF]
    rec_b[...] = wide_w[ROWS : ROWS + 1, 0:NF]
    conv_w[...] = pays[136 : 136 + KH, 0:C]
    conv_b[...] = pays[136 + KH : 137 + KH, 0:C]

    wait_bytes(red, N_WIDE - 1, sems.at[5])
    wait_bytes(raux, N_WIDE - 1, sems.at[1])
    wait_bytes(rdat, N_WIDE - 1, sems.at[0])
    wait_bytes(parts, N_REP - 1, sems.at[3])
    for kind in range(6):
        for g in range(CHUNKS):
            ring(kind, g).wait_send()


SPLIT_AT = 32


def local(
    pooled_emb, conv_weight, conv_bias, rec_weight, rec_bias, feat_cot, gram_cot, bag_ids,
    bag_lengths, field_table,
):
    vmem = pl.BlockSpec(memory_space=pltpu.VMEM)
    table, conv_w, conv_b, rec_w, rec_b = pl.pallas_call(
        whole_kernel,
        out_shape=(
            jax.ShapeDtypeStruct((NT, K, T_SHARE), f32),
            jax.ShapeDtypeStruct((KH, C), f32),
            jax.ShapeDtypeStruct((1, C), f32),
            jax.ShapeDtypeStruct((P_SIZE, C, NF), f32),
            jax.ShapeDtypeStruct((1, NF), f32),
        ),
        in_specs=[vmem] * 10,
        out_specs=(vmem,) * 5,
        scratch_shapes=[
            pltpu.VMEM((N_WIDE, MSG, 128), bf16),
            pltpu.VMEM((N_WIDE, 8, 128), f32),
            pltpu.VMEM((F * B_DEV, 128), f32),
            pltpu.VMEM((FPAD, LANES), f32),
            pltpu.VMEM((2 * RPAD, 128), f32),
            pltpu.VMEM((RPAD, K), f32),
            pltpu.VMEM((FT, LANES), f32),
            pltpu.VMEM((FT + 8, LANES), f32),
            pltpu.VMEM((B_DEV, 8, 128), i32),
            pltpu.VMEM((N_WIDE, 3, 128), f32),
            pltpu.VMEM((N_WIDE, MSG, 128), bf16),
            pltpu.VMEM((N_WIDE, 3, 128), f32),
            pltpu.VMEM((3, 128), f32),
            pltpu.VMEM((N_REP, 3, 128), f32),
            pltpu.VMEM((N_WIDE, 3, 128), f32),
            pltpu.VMEM((N_REP, CHUNKS, 2, BLOCK, 256), bf16),
            pltpu.VMEM((NT // 2 * K, 256), f32),
            pltpu.VMEM((192, 128), f32),
            pltpu.VMEM((RPAD, 128), f32),
            pltpu.SemaphoreType.DMA((GROUPS,)),
            pltpu.SemaphoreType.DMA((6, CHUNKS)),
            pltpu.SemaphoreType.DMA((6,)),
            pltpu.SemaphoreType.DMA((7,)),
        ],
        compiler_params=pltpu.CompilerParams(
            vmem_limit_bytes=VMEM_LIMIT, collective_id=0, has_side_effects=True
        ),
        name="whole",
    )(
        conv_weight.T, conv_bias.reshape(1, C), pooled_emb.transpose(1, 0, 2),
        feat_cot.transpose(0, 2, 1), gram_cot, rec_weight.transpose(1, 0, 2),
        rec_bias.reshape(1, NF), bag_ids.transpose(0, 2, 1), bag_lengths,
        field_table.reshape(1, F),
    )
    return table, conv_w.T, conv_b.reshape(C), rec_w.transpose(1, 0, 2), rec_b.reshape(NF)


def solution(mesh):
    in_specs = (
        P(("wide", "rep"), None, None), P(), P(), P(), P(), P(("wide", "rep"), None, None),
        P(("wide", "rep"), None, None), P(("wide", "rep"), None, None), P(("wide", "rep"), None),
        P(),
    )
    out_specs = (P(None, None, ("wide", "rep")), P(), P(), P(), P())
    return jax.shard_map(local, mesh=mesh, in_specs=in_specs, out_specs=out_specs, check_vma=False)
```

time: 1520 us -> 48.2 us (0.03); the launches traced: 1500 us -> 47.8 us
  other arithmetic: 1060 us -> 0 us
  local copies, waits for them, and re-layouts: 209 us -> 4.48 us
  blocking collectives: 185 us -> 0 us
  Pallas kernels: 0 us -> 42.6 us
  matrix products: 30 us -> 0 us
    scatter-add x64 -> x0, other arithmetic: 1040 us -> none  [add_block(): partial_value.at[target.reshape(-1)]]
    dynamic_slice x256 -> x0, local copies, waits for them, and re-layouts: 156 us -> none  [the longest x64 57.1 us: add_block(): grad_here = lax.dynamic_slice_in_dim(shard_grad, offset, block_rows, 0)]
    all_gather x2 -> x0, blocking collectives: 106 us -> none  [the longest x1 54.2 us: local(): lax.all_gather(bag_ids, 'wide', axis=0, tiled=True)]
    psum x1 -> x0, blocking collectives: 78.3 us -> none  [local(): dense_sums = lax.psum(dense_terms, ('wide', 'rep'))]
    pallas_call x0 -> x1, Pallas kernels: none -> 42.6 us  [local(): pl.pallas_call(whole_kernel, out_shape=(jax.ShapeDtypeStruct((NT, K, T_SH...]
    dot_general x13 -> x0, matrix products: 30 us -> none  [the longest x7 15.7 us: dense_backward(): jnp.einsum('c,bcik->bik', conv_weight[:, shift], window, precision=highest)]
    reshape x65 -> x0, local copies, waits for them, and re-layouts: 15.8 us -> none  [the longest x64 8.89 us: add_block(): target.reshape(-1)]
  transfers between devices with their start and end apart: 2 -> 0, of which waited for: 0 -> 0; matrix products, arithmetic and copies ran while one was open for 1% -> 0% of each run, Pallas kernels for 0% -> 0%
where the time goes in v2:
time: 48.2 us; the launch traced here: 47.8 us
  Pallas kernels  42.6 us (88%)
  local copies, waits for them, and re-layouts  4.48 us (9%)
  between operations  0.66 us (1%)
    pallas_call x1, Pallas kernels, local(): pl.pallas_call(whole_kernel, out_shape=(jax.ShapeDtypeStruct((NT, K, T_SH...  42.6 us
    unnamed x13, local copies, waits for them, and re-layouts  4.48 us

profile of v2, /device:TPU:1, one launch (start us, length us, event | category | flops | bytes accessed | tf_op | source)
XLA Modules:
  0.0 47.8 jit_solution(10920773543570061843)
XLA Ops:
  0.6 42.6 %whole.1 = (f32[26,64,128]{2,1,0:T(8,128)}, f32[7,14]{1,0:T(8,128)}, f32[1,14]{1,0:T(1,128)}, f32[19,14,57]{2,1,0:T(8,128)}, f32[1,57]{1,0:T(1,128)}) custom-call(f32[7,14]{1,0:T(8,128)} %bitcast.17, f32[1,14]{1,0:T(1,128)} %bitcast.19, bf16[39,8,64]{2,1,0:T(8,128)(2,1)} %bitcast.15, bf16[8,64,96]{2,1,0:T(8,128)(2,1)} %bitcast.14, bf16[8,96,96]{2,1,0:T(8,128)(2,1)} %gram.1, ...), custom_call_target="tpu_custom_call" | custom-call | tf_op jit(solution)/shard_map/whole/pallas_call | solution.py:440
  43.3 0.0 copy-start.1
  43.3 0.0 copy-start
  43.3 2.2 %copy.20 = f32[26,64,128]{2,1,0:T(8,128)} copy(f32[26,64,128]{2,1,0:T(8,128)} %get-tuple-element.20) | data formatting | bytes 1703936
  45.5 0.0 copy-done.1
  45.5 0.0 copy-start.3
  45.5 0.6 %copy.21 = f32[14,7]{0,1:T(8,128)} copy(f32[14,7]{0,1:T(8,128)S(1)} %bitcast.18) | data formatting | bytes 784
  46.1 0.0 copy-done.3
  46.1 0.5 %copy.22 = f32[14]{0:T(128)} copy(f32[14]{0:T(128)S(1)} %bitcast.23) | data formatting | bytes 112
  46.6 0.0 copy-done
  46.6 0.0 copy-start.2
  46.6 0.7 %copy.23 = f32[14,19,57]{2,0,1:T(8,128)} copy(f32[14,19,57]{2,0,1:T(8,128)S(1)} %bitcast.13) | data formatting | bytes 121296
  47.2 0.0 copy-done.2
  47.2 0.5 %copy.24 = f32[57]{0:T(128)} copy(f32[57]{0:T(128)S(1)} %bitcast.22) | data formatting | bytes 456
Async XLA Ops:
  43.3 2.2 %copy-start.1 = (f32[7,14]{1,0:T(8,128)S(1)}, f32[7,14]{1,0:T(8,128)}, u32[]{:S(2)}) copy-start(f32[7,14]{1,0:T(8,128)} %get-tuple-element.11) | copy-start | bytes 1180
  43.3 3.3 %copy-start = (f32[19,14,57]{2,1,0:T(8,128)S(1)}, f32[19,14,57]{2,1,0:T(8,128)}, u32[]{:S(2)}) copy-start(f32[19,14,57]{2,1,0:T(8,128)} %get-tuple-element.13) | copy-start | bytes 181948
  45.5 0.6 %copy-start.3 = (f32[1,14]{1,0:T(1,128)S(1)}, f32[1,14]{1,0:T(1,128)}, u32[]{:S(2)}) copy-start(f32[1,14]{1,0:T(1,128)} %get-tuple-element.12) | copy-start | bytes 172
  46.6 0.7 %copy-start.2 = (f32[1,57]{1,0:T(1,128)S(1)}, f32[1,57]{1,0:T(1,128)}, u32[]{:S(2)}) copy-start(f32[1,57]{1,0:T(1,128)} %get-tuple-element.14) | copy-start | bytes 688

commit v3 on v2

--- a/solution.py
+++ b/solution.py
@@ -29,6 +29,10 @@
 FPAD = 40
 BAGS = B_DEV * FPAD
 MSG = 24
+PARTNERS = sorted(
+    ((y, z, c) for y in range(4) for z in range(8) for c in range(2)),
+    key=lambda at: (min(at[0], 4 - at[0]) + min(at[1], 8 - at[1]), at),
+)
 GROUPS = 4
 CHUNKS = GROUPS + 1
 BLOCK = 72
@@ -61,8 +65,8 @@
 
 
 def dense_part(
-    me_w, cw, cb, emb, cot, gram, rw, rb, ids, lengths, field_table,
-    send, stage, es, xs, tz, rws, fs, fg, ip,
+    me, cw, cb, emb, cot, gram, rw, rb, ids, lengths, field_table, order,
+    send, stage, es, xs, tz, rws, fs, fg, ip, weight_terms,
 ):
     es[:, 0:K] = emb[...].astype(f32).reshape(F * B_DEV, K)
     for m in range(B_DEV // 2):
@@ -118,6 +122,7 @@
     )
     cg_s = split(conv_grad)
     emb_grad = fg[0:FPAD, :] + mm3(split(band.T), cg_s)
+    weight_terms(xb, pooled_s, recg_s, cg_s)
 
     low = iota((FPAD, 128), 1) < K
     lows, highs = [], []
@@ -139,15 +144,19 @@
         value = value + (pltpu.roll(wide, FPAD * s, 1) if s else wide)
     value = value[:, 0:BAGS] - 1
 
-    peer_at = iota((N_WIDE, BAGS), 0)
+    peer_at = jnp.broadcast_to(order[:, 0:1], (N_WIDE, BAGS))
+    index_at = iota((N_WIDE, BAGS), 0).astype(f32)
     values, offsets, owned = [], [], []
     count = jnp.zeros((N_WIDE, BAGS), f32)
     for j in range(BAG):
         v = value[j : j + 1, :]
-        o = jnp.where(v >= 0, ((v >> 9) - me_w) & (N_WIDE - 1), -1)
+        w = v >> 9
+        o = (((w >> 4) - me[0]) & 3) * 16 + (((w >> 1) - me[1]) & 7) * 2 + ((w - me[2]) & 1)
+        o = jnp.where(v >= 0, o, -1)
         hit = (peer_at == o).astype(f32)
         values.append(v)
-        offsets.append(o)
+        o = jnp.sum(hit * index_at, axis=0, keepdims=True).astype(i32)
+        offsets.append(jnp.where(v >= 0, o, -1))
         owned.append(hit)
         count = count + hit
     before = (iota((BAGS, BAGS), 0) < iota((BAGS, BAGS), 1)).astype(f32).astype(bf16)
@@ -186,7 +195,6 @@
     for c in range(GROUPS):
         rows = pick(iota((256, 2 * BAGS), 0) + 256 * c, near)
         send[16 * c : 16 * c + 16, 0:16, :] = rows.astype(bf16).reshape(16, 16, 128)
-    return xb, pooled_s, recg_s, cg_s
 
 
 def weight_part(xb, pooled_s, recg_s, cg_s, aux, tz):
@@ -205,11 +213,10 @@
     taps = jnp.where(lane < KH, taps, 0.0) + bias
     taps = jnp.concatenate([taps, jnp.zeros((128 - C, 128), f32)], axis=0).T[0:8]
     pay = jnp.concatenate([rec_term[0:136], rec_term[136:272]], axis=1)
-    aux[:, 0, :] = pay[0:64]
-    aux[:, 1, :] = pay[64:128]
-    aux[:, 2, :] = jnp.concatenate(
-        [pay[128:136], taps, jnp.zeros((N_WIDE - 16, 128), f32)], axis=0
-    )
+    aux[:, :, 0, :] = pay[0:64].reshape(8, 8, 128)
+    aux[:, :, 1, :] = pay[64:128].reshape(8, 8, 128)
+    last = jnp.concatenate([pay[128:136], taps, jnp.zeros((N_WIDE - 16, 128), f32)], axis=0)
+    aux[:, :, 2, :] = last.reshape(8, 8, 128)
 
 
 def windows(codes, first, width):
@@ -255,19 +262,21 @@
 
 
 def whole_kernel(
-    cw, cb, emb, cot, gram, rw, rb, ids, lengths, field_table,
-    table, conv_w, conv_b, rec_w, rec_b,
+    cw, cb, emb, cot, gram, rw, rb, ids, lengths, field_table, order,
+    acc, red,
     send, stage, es, xs, tz, rws, fs, fg, ip, aux,
-    rdat, raux, part, parts, red, vt, acc, pays, wide_w,
-    data_sems, ring_recv, ring_send, sems,
+    rdat, sums_a, sums_b, part_a, part_b, parts, vt,
+    data_sems, send_sems, ring_recv, ring_send, sems,
 ):
     me_w = lax.axis_index("wide")
     me_x = lax.axis_index("rep")
     right = lax.rem(me_x + 1, N_REP)
     left = lax.rem(me_x + N_REP - 1, N_REP)
-
-    def peer(o):
-        return lax.rem(me_w + o, N_WIDE)
+    me_line = (me_w // 16) * 2 + lax.rem(me_w, 2)
+    me_y, me_z, me_c = me_w // 16, lax.rem(me_w // 2, 8), lax.rem(me_w, 2)
+
+    def on_line(line, z):
+        return (line // 2) * 16 + z * 2 + lax.rem(line, 2)
 
     def wide_copy(src, dst, to, s, r):
         return pltpu.make_async_remote_copy(
@@ -286,53 +295,59 @@
 
     barrier = pltpu.get_barrier_semaphore()
 
-    def greet(o, carry):
-        pl.semaphore_signal(barrier, inc=1, device_id=(peer(o), me_x), device_id_type=MESH)
-        return carry
-
-    lax.fori_loop(1, N_WIDE, greet, 0)
+    def partner(o):
+        y, z, c = PARTNERS[o]
+        return lax.rem(me_y + y, 4) * 16 + lax.rem(me_z + z, 8) * 2 + lax.rem(me_c + c, 2)
+
+    for o in range(N_WIDE - 1, 0, -1):
+        pl.semaphore_signal(
+            barrier, inc=1, device_id=(partner(o), me_x), device_id_type=MESH
+        )
     for o in range(1, N_REP):
         pl.semaphore_signal(
             barrier, inc=1, device_id=(me_w, lax.rem(me_x + o, N_REP)), device_id_type=MESH
         )
 
-    terms = dense_part(
-        me_w, cw, cb, emb, cot, gram, rw, rb, ids, lengths, field_table,
+    def others(me, fn):
+        def go(o, carry):
+            fn(lax.rem(me + o, 8))
+            return carry
+
+        lax.fori_loop(1, 8, go, 0)
+
+    dense_part(
+        (me_y, me_z, me_c), cw, cb, emb, cot, gram, rw, rb, ids, lengths, field_table, order,
         send, stage, es, xs, tz, rws, fs, fg, ip,
+        lambda *terms: weight_part(*terms, aux, tz),
     )
     pl.semaphore_wait(barrier, N_WIDE - 1 + N_REP - 1)
-
-    def send_rows(o, carry):
-        wide_copy(
-            send.at[o], rdat.at[o], peer(o), sems.at[0], data_sems.at[o // 16]
-        ).start()
-        return carry
-
-    def send_terms(o, carry):
-        to = peer(o)
-        wide_copy(aux.at[to], raux.at[me_w], to, sems.at[1], sems.at[2]).start()
-        return carry
-
-    def send_sums(o, carry):
-        wide_copy(red.at[me_w], red.at[me_w], peer(o), sems.at[5], sems.at[6]).start()
-        return carry
-
-    lax.fori_loop(1, SPLIT_AT, send_rows, 0)
-    weight_part(*terms, aux, tz)
-    lax.fori_loop(1, N_WIDE, send_terms, 0)
-    lax.fori_loop(SPLIT_AT, N_WIDE, send_rows, 0)
+    others(me_line, lambda to: wide_copy(
+        aux.at[to], sums_a.at[me_line], on_line(to, me_z), sems.at[0], sems.at[1]
+    ).start())
+    sums_a[me_line] = aux[me_line]
+
+    for g in ISSUE:
+        for o in range(max(1, 16 * g), 16 * g + 16):
+            wide_copy(
+                send.at[o], rdat.at[o], partner(o), send_sems.at[0], data_sems.at[g]
+            ).start()
+    wait_bytes(sums_a, 7, sems.at[1])
+    part_a[...] = jnp.sum(sums_a[...], axis=0)
+    others(me_z, lambda to: wide_copy(
+        part_a.at[to], sums_b.at[me_z], on_line(me_line, to), sems.at[2], sems.at[3]
+    ).start())
+    sums_b[me_z] = part_a[me_z]
     rdat[0] = send[0]
-    raux[me_w] = aux[me_w]
     acc[...] = jnp.zeros(acc.shape, f32)
 
     def ring(kind, g):
-        slot, h, to, there = (
-            (0, 0, right, 1), (0, 1, right, 1), (0, 1, left, 2), (0, 0, left, 2),
-            (1, 0, right, 3), (2, 1, left, 3),
-        )[kind]
-        return rep_copy(
-            vt.at[slot, g, h], vt.at[there, g, h], to, ring_send.at[kind], ring_recv.at[kind, g]
-        )
+        if kind < 2:
+            to, there = ((right, 1), (left, 2))[kind]
+            src, dst = vt.at[0, g], vt.at[there, g]
+        else:
+            slot, h, to = ((1, 0, right), (2, 1, left))[kind - 2]
+            src, dst = vt.at[slot, g, h], vt.at[3, g, h]
+        return rep_copy(src, dst, to, ring_send.at[kind], ring_recv.at[kind, g])
 
     def step(g, carry):
         @pl.when(g < GROUPS)
@@ -358,60 +373,89 @@
 
         @pl.when(g < CHUNKS)
         def _():
-            for kind in (0, 2, 1, 3):
+            for kind in (0, 1):
                 ring(kind, g).start()
 
-        @pl.when((g >= 1) & (g <= CHUNKS))
-        def _():
-            ring(0, g - 1).wait_recv()
-            ring(4, g - 1).start()
-            ring(2, g - 1).wait_recv()
-            ring(5, g - 1).start()
-
-        @pl.when(g < CHUNKS)
-        def _():
-            add_rows(me_x, vt, acc, 0, g)
-
-        @pl.when(g == 2)
-        def _():
-            wait_bytes(raux, N_WIDE - 1, sems.at[2])
-            part[...] = jnp.sum(raux[...], axis=0)
+        @pl.when((g >= ON) & (g < CHUNKS + ON))
+        def _():
+            ring(0, g - ON).wait_recv()
+            ring(2, g - ON).start()
+            ring(1, g - ON).wait_recv()
+            ring(3, g - ON).start()
+
+        @pl.when(g == AR[0])
+        def _():
+            wait_bytes(sums_b, 7, sems.at[3])
+            part_b[...] = jnp.sum(sums_b[...], axis=0)
             for o in range(1, N_REP):
                 to = lax.rem(me_x + o, N_REP)
-                rep_copy(part, parts.at[me_x], to, sems.at[3], sems.at[4]).start()
-            parts[me_x] = part[...]
-
-        @pl.when((g >= 1) & (g <= CHUNKS))
-        def _():
-            ring(1, g - 1).wait_recv()
-            ring(3, g - 1).wait_recv()
-            add_rows(me_x, vt, acc, 1, g - 1)
-            add_rows(me_x, vt, acc, 2, g - 1)
-
-        @pl.when(g == 2)
-        def _():
-            wait_bytes(parts, N_REP - 1, sems.at[4])
-            red[me_w] = (parts[0] + parts[1]) + (parts[2] + parts[3])
-            lax.fori_loop(1, N_WIDE, send_sums, 0)
-
-        @pl.when(g >= 2)
-        def _():
-            ring(4, g - 2).wait_recv()
-            ring(5, g - 2).wait_recv()
-            add_rows(me_x, vt, acc, 3, g - 2)
+                rep_copy(part_b, parts.at[me_x], to, sems.at[4], sems.at[5]).start()
+            parts[me_x] = part_b[...]
+
+        @pl.when(g == AR[1])
+        def _():
+            wait_bytes(parts, N_REP - 1, sems.at[5])
+            red[me_line, me_z] = (parts[0] + parts[1]) + (parts[2] + parts[3])
+            others(me_z, lambda to: wide_copy(
+                red.at[me_line, me_z], red.at[me_line, me_z], on_line(me_line, to),
+                sems.at[6], sems.at[7],
+            ).start())
+
+        @pl.when(g == AR[2])
+        def _():
+            wait_bytes(sums_b, 7, sems.at[7])
+            others(me_line, lambda to: wide_copy(
+                red.at[me_line], red.at[me_line], on_line(to, me_z), sems.at[8], sems.at[9]
+            ).start())
+
+        @pl.when(g < CHUNKS)
+        def _():
+            add_rows(me_x, vt, acc, 0, g)
+
+        @pl.when((g >= ON) & (g < CHUNKS + ON))
+        def _():
+            add_rows(me_x, vt, acc, 1, g - ON)
+            add_rows(me_x, vt, acc, 2, g - ON)
+
+        @pl.when(g >= END)
+        def _():
+            ring(2, g - END).wait_recv()
+            ring(3, g - END).wait_recv()
+            add_rows(me_x, vt, acc, 3, g - END)
 
         return carry
 
-    lax.fori_loop(0, CHUNKS + 2, step, 0)
-
+    lax.fori_loop(0, CHUNKS + END, step, 0)
+
+    wait_bytes(red, 7, sems.at[9])
+    wait_bytes(red, 7, sems.at[8])
+    wait_bytes(sums_b, 7, sems.at[6])
+    wait_bytes(parts, N_REP - 1, sems.at[4])
+    wait_bytes(sums_b, 7, sems.at[2])
+    wait_bytes(sums_a, 7, sems.at[0])
+    wait_bytes(rdat, N_WIDE - 1, send_sems.at[0])
+    for kind in range(4):
+        for g in range(CHUNKS):
+            ring(kind, g).wait_send()
+
+
+ISSUE = (0, 1, 2, 3)
+AR = (1, 2, 4)
+ON = 1
+END = 2
+
+
+def results_kernel(acc, red, table, conv_w, conv_b, rec_w, rec_b, pays, wide_w, sems):
+    copies = []
     for t in range(NT):
         half = (t % 2) * T_SHARE
-        table[t] = acc[(t // 2) * K : (t // 2) * K + K, half : half + T_SHARE]
-
-    wait_bytes(red, N_WIDE - 1, sems.at[6])
+        copies.append(pltpu.make_async_copy(
+            acc.at[pl.ds((t // 2) * K, K), pl.ds(half, T_SHARE)], table.at[t], sems.at[t]
+        ))
+        copies[-1].start()
     scale = 1.0 / math.sqrt(SAMPLES)
     for g in range(3):
-        pays[64 * g : 64 * g + 64, :] = red[:, g, :] * scale
+        pays[64 * g : 64 * g + 64, :] = red[:, :, g, :].reshape(64, 128) * scale
     wide_w[0:136, :] = pays[0:136, :]
     wide_w[136:272, :] = pltpu.roll(pays[0:136, :], K, 1)
     for p in range(P_SIZE):
@@ -419,17 +463,8 @@
     rec_b[...] = wide_w[ROWS : ROWS + 1, 0:NF]
     conv_w[...] = pays[136 : 136 + KH, 0:C]
     conv_b[...] = pays[136 + KH : 137 + KH, 0:C]
-
-    wait_bytes(red, N_WIDE - 1, sems.at[5])
-    wait_bytes(raux, N_WIDE - 1, sems.at[1])
-    wait_bytes(rdat, N_WIDE - 1, sems.at[0])
-    wait_bytes(parts, N_REP - 1, sems.at[3])
-    for kind in range(6):
-        for g in range(CHUNKS):
-            ring(kind, g).wait_send()
-
-
-SPLIT_AT = 32
+    for copy in copies:
+        copy.wait()
 
 
 def local(
@@ -437,17 +472,15 @@
     bag_lengths, field_table,
 ):
     vmem = pl.BlockSpec(memory_space=pltpu.VMEM)
-    table, conv_w, conv_b, rec_w, rec_b = pl.pallas_call(
+    order = jnp.asarray([[16 * y + 2 * z + c] * 128 for y, z, c in PARTNERS], i32)
+    acc, red = pl.pallas_call(
         whole_kernel,
         out_shape=(
-            jax.ShapeDtypeStruct((NT, K, T_SHARE), f32),
-            jax.ShapeDtypeStruct((KH, C), f32),
-            jax.ShapeDtypeStruct((1, C), f32),
-            jax.ShapeDtypeStruct((P_SIZE, C, NF), f32),
-            jax.ShapeDtypeStruct((1, NF), f32),
+            pltpu.VMEM((NT // 2 * K, 256), f32),
+            pltpu.VMEM((8, 8, 3, 128), f32),
         ),
-        in_specs=[vmem] * 10,
-        out_specs=(vmem,) * 5,
+        in_specs=[vmem] * 11,
+        out_specs=(vmem,) * 2,
         scratch_shapes=[
             pltpu.VMEM((N_WIDE, MSG, 128), bf16),
             pltpu.VMEM((N_WIDE, 8, 128), f32),
@@ -458,20 +491,19 @@
             pltpu.VMEM((FT, LANES), f32),
             pltpu.VMEM((FT + 8, LANES), f32),
             pltpu.VMEM((B_DEV, 8, 128), i32),
-            pltpu.VMEM((N_WIDE, 3, 128), f32),
+            pltpu.VMEM((8, 8, 3, 128), f32),
             pltpu.VMEM((N_WIDE, MSG, 128), bf16),
-            pltpu.VMEM((N_WIDE, 3, 128), f32),
+            pltpu.VMEM((8, 8, 3, 128), f32),
+            pltpu.VMEM((8, 3, 128), f32),
+            pltpu.VMEM((8, 3, 128), f32),
             pltpu.VMEM((3, 128), f32),
             pltpu.VMEM((N_REP, 3, 128), f32),
-            pltpu.VMEM((N_WIDE, 3, 128), f32),
             pltpu.VMEM((N_REP, CHUNKS, 2, BLOCK, 256), bf16),
-            pltpu.VMEM((NT // 2 * K, 256), f32),
-            pltpu.VMEM((192, 128), f32),
-            pltpu.VMEM((RPAD, 128), f32),
             pltpu.SemaphoreType.DMA((GROUPS,)),
-            pltpu.SemaphoreType.DMA((6, CHUNKS)),
-            pltpu.SemaphoreType.DMA((6,)),
-            pltpu.SemaphoreType.DMA((7,)),
+            pltpu.SemaphoreType.DMA((1,)),
+            pltpu.SemaphoreType.DMA((4, CHUNKS)),
+            pltpu.SemaphoreType.DMA((4,)),
+            pltpu.SemaphoreType.DMA((10,)),
         ],
         compiler_params=pltpu.CompilerParams(
             vmem_limit_bytes=VMEM_LIMIT, collective_id=0, has_side_effects=True
@@ -481,8 +513,28 @@
         conv_weight.T, conv_bias.reshape(1, C), pooled_emb.transpose(1, 0, 2),
         feat_cot.transpose(0, 2, 1), gram_cot, rec_weight.transpose(1, 0, 2),
         rec_bias.reshape(1, NF), bag_ids.transpose(0, 2, 1), bag_lengths,
-        field_table.reshape(1, F),
+        field_table.reshape(1, F), order,
     )
+    acc = pltpu.with_memory_space_constraint(acc, pltpu.VMEM)
+    red = pltpu.with_memory_space_constraint(red, pltpu.VMEM)
+    table, conv_w, conv_b, rec_w, rec_b = pl.pallas_call(
+        results_kernel,
+        out_shape=(
+            jax.ShapeDtypeStruct((NT, K, T_SHARE), f32),
+            jax.ShapeDtypeStruct((KH, C), f32),
+            jax.ShapeDtypeStruct((1, C), f32),
+            jax.ShapeDtypeStruct((P_SIZE, C, NF), f32),
+            jax.ShapeDtypeStruct((1, NF), f32),
+        ),
+        in_specs=[vmem] * 2,
+        out_specs=(pl.BlockSpec(memory_space=pl.ANY),) + (vmem,) * 4,
+        scratch_shapes=[
+            pltpu.VMEM((192, 128), f32),
+            pltpu.VMEM((RPAD, 128), f32),
+            pltpu.SemaphoreType.DMA((NT,)),
+        ],
+        name="results",
+    )(acc, red)
     return table, conv_w.T, conv_b.reshape(C), rec_w.transpose(1, 0, 2), rec_b.reshape(NF)
 
 

time: 48.2 us -> 42 us (0.87)
  local copies, waits for them, and re-layouts: 4.48 us -> 0 us
  Pallas kernels: 42.6 us -> 41.3 us
    unnamed x13 -> x0, local copies, waits for them, and re-layouts: 4.48 us -> none
    pallas_call x1 -> x2, Pallas kernels: 42.6 us -> 41.3 us  [the longest x1 39.4 us: local(): pl.pallas_call(whole_kernel, out_shape=(pltpu.VMEM((NT // 2 * K, 256), f3...]
where the time goes in v3:
time: 42 us; the launch traced here: 41.9 us
  Pallas kernels  41.3 us (98%)
  between operations  0.64 us (2%)
    pallas_call x1, Pallas kernels, local(): pl.pallas_call(whole_kernel, out_shape=(pltpu.VMEM((NT // 2 * K, 256), f3...  39.4 us
    pallas_call x1, Pallas kernels, local(): pl.pallas_call(results_kernel, out_shape=(jax.ShapeDtypeStruct((NT, K, T_...  1.87 us

profile of v3, /device:TPU:1, one launch (start us, length us, event | category | flops | bytes accessed | tf_op | source)
XLA Modules:
  0.0 41.9 jit_solution(11666024300677876214)
XLA Ops:
  0.6 39.4 %whole.1 = (f32[832,256]{1,0:T(8,128)S(1)}, f32[8,8,3,128]{3,2,1,0:T(4,128)S(1)}) custom-call(f32[7,14]{1,0:T(8,128)} %bitcast.16, f32[1,14]{1,0:T(1,128)} %bitcast.17, bf16[39,8,64]{2,1,0:T(8,128)(2,1)} %bitcast.14, bf16[8,64,96]{2,1,0:T(8,128)(2,1)} %bitcast.13, bf16[8,96,96]{2,1,0:T(8,128)(2,1)} %gram.1, f32[19,14,57]{2,1,0:T(8,128)} %bitcast.12, ...), custom_call_target="tpu_custom_call" | custom-call | tf_op jit(solution)/shard_map/whole/pallas_call | solution.py:476
  40.0 1.9 %results.1 = (f32[26,64,128]{2,1,0:T(8,128)}, f32[7,14]{1,0:T(8,128)}, f32[1,14]{1,0:T(1,128)}, f32[19,14,57]{2,1,0:T(8,128)}, f32[1,57]{1,0:T(1,128)}) custom-call(f32[832,256]{1,0:T(8,128)S(1)} %get-tuple-element.12.acc, f32[8,8,3,128]{3,2,1,0:T(4,128)S(1)} %get-tuple-element.13.red), custom_call_target="tpu_custom_call" | custom-call | tf_op jit(solution)/shard_map/results/pallas_call | solution.py:520

commit v4 on v3

--- a/solution.py
+++ b/solution.py
@@ -35,7 +35,7 @@
 )
 GROUPS = 4
 CHUNKS = GROUPS + 1
-BLOCK = 72
+BLOCK = 2 * K + 8
 MESH = pl.DeviceIdType.MESH
 VMEM_LIMIT = 56 * 1024 * 1024
 f32 = jnp.float32
@@ -236,20 +236,21 @@
 
 
 def fill_chunk(vt, g, rows, codes, starts, width):
-    turned = rows.T
     row_at = iota((8, 256), 0)
+    meta = jnp.zeros((8, 256), f32)
     for h in range(2):
-        first = windows(codes, starts[h], width)
-        second = windows(codes, 64 + starts[h], width)
-        meta = jnp.where(row_at == 0, first, jnp.where(row_at == 1, second, 0.0))
-        vt[0, g, h] = jnp.concatenate([turned[K * h : K * h + K], meta], axis=0).astype(bf16)
+        for part in range(2):
+            line = windows(codes, 64 * part + starts[h], width)
+            meta = jnp.where(row_at == 2 * h + part, line, meta)
+    vt[0, g] = jnp.concatenate([rows.T, meta], axis=0).astype(bf16)
 
 
 def add_rows(me_x, vt, acc, slot, g):
-    meta = [vt[slot, g, h][K:BLOCK].astype(f32) for h in range(2)]
-    rows = jnp.concatenate([vt[slot, g, h][0:K] for h in range(2)], axis=1)
-    code = jnp.concatenate([m[0:1] for m in meta], axis=1).astype(i32) - 1
-    place = jnp.concatenate([m[1:2] for m in meta], axis=1).astype(i32)
+    block = vt[slot, g]
+    meta = block[2 * K :].astype(f32)
+    rows = jnp.concatenate([block[0:K], block[K : 2 * K]], axis=1)
+    code = jnp.concatenate([meta[0:1], meta[2:3]], axis=1).astype(i32) - 1
+    place = jnp.concatenate([meta[1:2], meta[3:4]], axis=1).astype(i32)
     table_at = code >> 2
     mine = (code >= 0) & ((code & 3) == me_x)
     target = jnp.where(mine, (table_at & 1) * T_SHARE + place, -1)
@@ -258,7 +259,7 @@
     spread = jnp.concatenate(
         [rows * (pair_at == t).astype(f32).astype(bf16) for t in range(NT // 2)], axis=0
     )
-    acc[...] += mm(spread, hits, NT_DIMS)
+    acc[...] += mm(spread, hits, NT_DIMS).reshape(acc.shape)
 
 
 def whole_kernel(
@@ -321,22 +322,16 @@
         lambda *terms: weight_part(*terms, aux, tz),
     )
     pl.semaphore_wait(barrier, N_WIDE - 1 + N_REP - 1)
-    others(me_line, lambda to: wide_copy(
-        aux.at[to], sums_a.at[me_line], on_line(to, me_z), sems.at[0], sems.at[1]
-    ).start())
-    sums_a[me_line] = aux[me_line]
 
     for g in ISSUE:
         for o in range(max(1, 16 * g), 16 * g + 16):
             wide_copy(
                 send.at[o], rdat.at[o], partner(o), send_sems.at[0], data_sems.at[g]
             ).start()
-    wait_bytes(sums_a, 7, sems.at[1])
-    part_a[...] = jnp.sum(sums_a[...], axis=0)
-    others(me_z, lambda to: wide_copy(
-        part_a.at[to], sums_b.at[me_z], on_line(me_line, to), sems.at[2], sems.at[3]
+    others(me_line, lambda to: wide_copy(
+        aux.at[to], sums_a.at[me_line], on_line(to, me_z), sems.at[0], sems.at[1]
     ).start())
-    sums_b[me_z] = part_a[me_z]
+    sums_a[me_line] = aux[me_line]
     rdat[0] = send[0]
     acc[...] = jnp.zeros(acc.shape, f32)
 
@@ -345,8 +340,8 @@
             to, there = ((right, 1), (left, 2))[kind]
             src, dst = vt.at[0, g], vt.at[there, g]
         else:
-            slot, h, to = ((1, 0, right), (2, 1, left))[kind - 2]
-            src, dst = vt.at[slot, g, h], vt.at[3, g, h]
+            slot, rows, to = ((1, pl.ds(0, K), right), (2, pl.ds(K, BLOCK - K), left))[kind - 2]
+            src, dst = vt.at[slot, g, rows], vt.at[3, g, rows]
         return rep_copy(src, dst, to, ring_send.at[kind], ring_recv.at[kind, g])
 
     def step(g, carry):
@@ -365,16 +360,18 @@
             codes = got[:, 16:24, :].astype(f32)[:, 4, :]
             fill_chunk(vt, g, rows, codes, (0, 16), 16)
 
-        @pl.when(g == GROUPS)
+        @pl.when(g < GROUPS)
+        def _():
+            for kind in (0, 1):
+                ring(kind, g).start()
+
+        @pl.when(g == GROUPS - 1)
         def _():
             tail = rdat[:, 16:24, :].astype(f32)
             rows = tail[:, 0:4, :].reshape(256, 128)
             fill_chunk(vt, GROUPS, rows, tail[:, 4, :], (32, 36), 4)
-
-        @pl.when(g < CHUNKS)
-        def _():
             for kind in (0, 1):
-                ring(kind, g).start()
+                ring(kind, GROUPS).start()
 
         @pl.when((g >= ON) & (g < CHUNKS + ON))
         def _():
@@ -382,6 +379,15 @@
             ring(2, g - ON).start()
             ring(1, g - ON).wait_recv()
             ring(3, g - ON).start()
+
+        @pl.when(g == AR[3])
+        def _():
+            wait_bytes(sums_a, 7, sems.at[1])
+            part_a[...] = jnp.sum(sums_a[...], axis=0)
+            others(me_z, lambda to: wide_copy(
+                part_a.at[to], sums_b.at[me_z], on_line(me_line, to), sems.at[2], sems.at[3]
+            ).start())
+            sums_b[me_z] = part_a[me_z]
 
         @pl.when(g == AR[0])
         def _():
@@ -439,18 +445,17 @@
             ring(kind, g).wait_send()
 
 
-ISSUE = (0, 1, 2, 3)
-AR = (1, 2, 4)
+ISSUE = (0, 1, 3, 2)
+AR = (1, 2, 4, 0)
 ON = 1
 END = 2
 
 
 def results_kernel(acc, red, table, conv_w, conv_b, rec_w, rec_b, pays, wide_w, sems):
     copies = []
-    for t in range(NT):
-        half = (t % 2) * T_SHARE
+    for half in range(2):
         copies.append(pltpu.make_async_copy(
-            acc.at[pl.ds((t // 2) * K, K), pl.ds(half, T_SHARE)], table.at[t], sems.at[t]
+            acc.at[:, :, pl.ds(half * T_SHARE, T_SHARE)], table.at[:, half], sems.at[half]
         ))
         copies[-1].start()
     scale = 1.0 / math.sqrt(SAMPLES)
@@ -476,7 +481,7 @@
     acc, red = pl.pallas_call(
         whole_kernel,
         out_shape=(
-            pltpu.VMEM((NT // 2 * K, 256), f32),
+            pltpu.VMEM((NT // 2, K, 256), f32),
             pltpu.VMEM((8, 8, 3, 128), f32),
         ),
         in_specs=[vmem] * 11,
@@ -498,7 +503,7 @@
             pltpu.VMEM((8, 3, 128), f32),
             pltpu.VMEM((3, 128), f32),
             pltpu.VMEM((N_REP, 3, 128), f32),
-            pltpu.VMEM((N_REP, CHUNKS, 2, BLOCK, 256), bf16),
+            pltpu.VMEM((N_REP, CHUNKS, BLOCK, 256), bf16),
             pltpu.SemaphoreType.DMA((GROUPS,)),
             pltpu.SemaphoreType.DMA((1,)),
             pltpu.SemaphoreType.DMA((4, CHUNKS)),
@@ -520,7 +525,7 @@
     table, conv_w, conv_b, rec_w, rec_b = pl.pallas_call(
         results_kernel,
         out_shape=(
-            jax.ShapeDtypeStruct((NT, K, T_SHARE), f32),
+            jax.ShapeDtypeStruct((NT // 2, 2, K, T_SHARE), f32),
             jax.ShapeDtypeStruct((KH, C), f32),
             jax.ShapeDtypeStruct((1, C), f32),
             jax.ShapeDtypeStruct((P_SIZE, C, NF), f32),
@@ -531,10 +536,11 @@
         scratch_shapes=[
             pltpu.VMEM((192, 128), f32),
             pltpu.VMEM((RPAD, 128), f32),
-            pltpu.SemaphoreType.DMA((NT,)),
+            pltpu.SemaphoreType.DMA((2,)),
         ],
         name="results",
     )(acc, red)
+    table = table.reshape(NT, K, T_SHARE)
     return table, conv_w.T, conv_b.reshape(C), rec_w.transpose(1, 0, 2), rec_b.reshape(NF)
 
 

time: 42 us -> 41.7 us (level)
  Pallas kernels: 41.3 us -> 40.8 us
    pallas_call x2, Pallas kernels: 41.3 us -> 40.8 us  [the longest x1 39.2 us: local(): pl.pallas_call(whole_kernel, out_shape=(pltpu.VMEM((NT // 2, K, 256), f32...]
where the time goes in v4:
time: 41.7 us; the launch traced here: 41.5 us
  Pallas kernels  40.8 us (98%)
  between operations  0.64 us (2%)
    pallas_call x1, Pallas kernels, local(): pl.pallas_call(whole_kernel, out_shape=(pltpu.VMEM((NT // 2, K, 256), f32...  39.2 us
    pallas_call x1, Pallas kernels, local(): pl.pallas_call(results_kernel, out_shape=(jax.ShapeDtypeStruct((NT // 2,...  1.59 us

profile of v4, /device:TPU:1, one launch (start us, length us, event | category | flops | bytes accessed | tf_op | source)
XLA Modules:
  0.0 41.5 jit_solution(19662049978115853)
XLA Ops:
  0.6 39.2 %whole.1 = (f32[13,64,256]{2,1,0:T(8,128)S(1)}, f32[8,8,3,128]{3,2,1,0:T(4,128)S(1)}) custom-call(f32[7,14]{1,0:T(8,128)} %bitcast.17, f32[1,14]{1,0:T(1,128)} %bitcast.18, bf16[39,8,64]{2,1,0:T(8,128)(2,1)} %bitcast.15, bf16[8,64,96]{2,1,0:T(8,128)(2,1)} %bitcast.14, bf16[8,96,96]{2,1,0:T(8,128)(2,1)} %gram.1, f32[19,14,57]{2,1,0:T(8,128)} %bitcast.13, ...), custom_call_target="tpu_custom_call" | custom-call | tf_op jit(solution)/shard_map/whole/pallas_call | solution.py:481
  39.9 1.6 %results.1 = (f32[13,2,64,128]{3,2,1,0:T(8,128)}, f32[7,14]{1,0:T(8,128)}, f32[1,14]{1,0:T(1,128)}, f32[19,14,57]{2,1,0:T(8,128)}, f32[1,57]{1,0:T(1,128)}) custom-call(f32[13,64,256]{2,1,0:T(8,128)S(1)} %get-tuple-element.12.acc, f32[8,8,3,128]{3,2,1,0:T(4,128)S(1)} %get-tuple-element.13.red), custom_call_target="tpu_custom_call" | custom-call | tf_op jit(solution)/shard_map/results/pallas_call | solution.py:525

commit v5 on v4

--- a/solution.py
+++ b/solution.py
@@ -68,7 +68,7 @@
     me, cw, cb, emb, cot, gram, rw, rb, ids, lengths, field_table, order,
     send, stage, es, xs, tz, rws, fs, fg, ip, weight_terms,
 ):
-    es[:, 0:K] = emb[...].astype(f32).reshape(F * B_DEV, K)
+    es[0 : F * B_DEV, 0:K] = emb[...].astype(f32).reshape(F * B_DEV, K)
     for m in range(B_DEV // 2):
         pair = [es[pl.ds(2 * m + e, F, stride=B_DEV), :][:, 0:K] for e in range(2)]
         xs[0:F, 128 * m : 128 * m + 128] = jnp.concatenate(pair, axis=1)
@@ -489,7 +489,7 @@
         scratch_shapes=[
             pltpu.VMEM((N_WIDE, MSG, 128), bf16),
             pltpu.VMEM((N_WIDE, 8, 128), f32),
-            pltpu.VMEM((F * B_DEV, 128), f32),
+            pltpu.VMEM((FPAD * B_DEV, 128), f32),
             pltpu.VMEM((FPAD, LANES), f32),
             pltpu.VMEM((2 * RPAD, 128), f32),
             pltpu.VMEM((RPAD, K), f32),

time: 41.7 us -> 41.8 us (level)
  no operation moved by 1% of the time
where the time goes in v5:
time: 41.8 us; the launch traced here: 41.5 us
  Pallas kernels  40.8 us (98%)
  between operations  0.64 us (2%)
    pallas_call x1, Pallas kernels, local(): pl.pallas_call(whole_kernel, out_shape=(pltpu.VMEM((NT // 2, K, 256), f32...  39.2 us
    pallas_call x1, Pallas kernels, local(): pl.pallas_call(results_kernel, out_shape=(jax.ShapeDtypeStruct((NT // 2,...  1.59 us

profile of v5, /device:TPU:1, one launch (start us, length us, event | category | flops | bytes accessed | tf_op | source)
XLA Modules:
  0.0 41.5 jit_solution(15254838806762543153)
XLA Ops:
  0.6 39.2 %whole.1 = (f32[13,64,256]{2,1,0:T(8,128)S(1)}, f32[8,8,3,128]{3,2,1,0:T(4,128)S(1)}) custom-call(f32[7,14]{1,0:T(8,128)} %bitcast.17, f32[1,14]{1,0:T(1,128)} %bitcast.18, bf16[39,8,64]{2,1,0:T(8,128)(2,1)} %bitcast.15, bf16[8,64,96]{2,1,0:T(8,128)(2,1)} %bitcast.14, bf16[8,96,96]{2,1,0:T(8,128)(2,1)} %gram.1, f32[19,14,57]{2,1,0:T(8,128)} %bitcast.13, ...), custom_call_target="tpu_custom_call" | custom-call | tf_op jit(solution)/shard_map/whole/pallas_call | solution.py:481
  39.9 1.6 %results.1 = (f32[13,2,64,128]{3,2,1,0:T(8,128)}, f32[7,14]{1,0:T(8,128)}, f32[1,14]{1,0:T(1,128)}, f32[19,14,57]{2,1,0:T(8,128)}, f32[1,57]{1,0:T(1,128)}) custom-call(f32[13,64,256]{2,1,0:T(8,128)S(1)} %get-tuple-element.12.acc, f32[8,8,3,128]{3,2,1,0:T(4,128)S(1)} %get-tuple-element.13.red), custom_call_target="tpu_custom_call" | custom-call | tf_op jit(solution)/shard_map/results/pallas_call | solution.py:525
